TPU v7x, 32 devices: a whole 2x2x4 slice. The times are simulated.
32 devices in a mesh: batch: 16 (over z, x, core), seq: 2 (over y).
Axes of the slice: x: 2, y: 2, z: 4, core: 2. Of those that a mesh axis runs over, the one named last changes fastest.
Arguments:
- tokens: bfloat16 [16, 2048, 768], P('batch', 'seq'), may hold values from -6 to 6
- cotangent: bfloat16 [16, 2048, 768], P('batch', 'seq'), may hold values from -6 to 6
- segments: int32 [16, 2048], P('batch'), may hold values from 0 to 3, as said below
- adapter_index: int32 [16, 1], P('batch'), may hold values from 0 to 3
- qkv_weight: bfloat16 [1, 3, 768, 768], P(None, None, ('batch', 'seq')), may hold values from -0.21875 to 0.21875
- out_weight: bfloat16 [1, 768, 768], P(None, ('batch', 'seq')), may hold values from -0.875 to 0.875
- ffn_in_weight: bfloat16 [1, 2, 768, 3072], P(None, None, ('batch', 'seq')), may hold values from -0.21875 to 0.21875
- ffn_out_weight: bfloat16 [1, 3072, 768], P(None, ('batch', 'seq')), may hold values from -0.109375 to 0.109375
- norm_gain: float32 [1, 2, 768], replicated, may hold values from 0.1 to 1.9
- norm_bias: float32 [1, 2, 768], replicated, may hold values from -2 to 2
- adapt_in: bfloat16 [1, 4, 6, 768, 16], replicated, may hold values from -0.21875 to 0.21875
- adapt_down: bfloat16 [1, 4, 3072, 16], replicated, may hold values from -0.109375 to 0.109375
- adapt_out: bfloat16 [1, 4, 5, 16, 768], replicated, may hold values from -1.5 to 1.5
- adapt_ffn: bfloat16 [1, 4, 2, 16, 3072], replicated, may hold values from -1.5 to 1.5
Outputs:
- mixed: bfloat16 [16, 2048, 768], P('batch', 'seq')
- input_grad: bfloat16 [16, 2048, 768], P('batch', 'seq')
- grad_adapt_in: float32 [1, 4, 6, 768, 16], replicated
- grad_adapt_down: float32 [1, 4, 3072, 16], replicated
- grad_adapt_out: float32 [1, 4, 5, 16, 768], replicated
- grad_adapt_ffn: float32 [1, 4, 2, 16, 3072], replicated
Inputs may be any that keep to these rules, and one draw needn't show every extreme that they name: `segments`: document numbers start at 0 in each sequence and rise by one at each new document; every sequence holds exactly 4 documents, one of which starts before position 1024 and ends at or after position 1024. `adapter_index`: every adapter is used by some sequence.
All inputs are finite; a program needn't handle non-finite values.
Results may differ from a plain program's by a relative error of at most 0.023.
The roundings to bfloat16 on the way count: a program that leaves them out, or rounds other values in their place, can miss the bound.
Values may be sent and summed in bfloat16 or wider, within the bound.
A program may use at most 320 MiB of HBM per device.

v0:
```python
import math

import jax
import jax.numpy as jnp
from jax import lax
from jax.sharding import PartitionSpec as P

HEADS = 12
HEAD_DIM = 64
ADAPTERS = 4
LAYERS = 1
HALF = 512


EPSILON = 1e-06
ROPE_BASE = 1000.0
PRECISE = lax.Precision.HIGHEST


def shifted(array, axis, by):
    count = lax.axis_size(axis)
    pairs = [(i, i + by) for i in range(count) if 0 <= i + by < count]
    return lax.ppermute(array, axis, pairs)


def doc_positions(segment_ids):
    position_ids = jnp.arange(segment_ids.shape[-1], dtype=jnp.int32)
    starts_here = jnp.concatenate(
        [
            jnp.ones(segment_ids.shape[:-1] + (1,), dtype=jnp.bool_),
            segment_ids[..., 1:] != segment_ids[..., :-1],
        ],
        axis=-1,
    )
    doc_start = lax.cummax(jnp.where(starts_here, position_ids, 0), axis=segment_ids.ndim - 1)
    return (position_ids - doc_start).astype(jnp.float32)


def rope_tables(segment_ids):
    positions = doc_positions(segment_ids)
    frequency = jnp.power(ROPE_BASE, -2.0 * jnp.arange(HEAD_DIM // 2, dtype=jnp.float32) / HEAD_DIM)
    angles = positions[..., None] * frequency
    return (jnp.cos(angles), jnp.sin(angles))


def rotate(vectors, cosine_table, sine_table):
    half_dim = vectors.shape[-1] // 2
    first_half = vectors[..., :half_dim]
    second_half = vectors[..., half_dim:]
    cosine_rows = cosine_table[..., None, :]
    sine_rows = sine_table[..., None, :]
    return jnp.concatenate(
        [
            first_half * cosine_rows - second_half * sine_rows,
            second_half * cosine_rows + first_half * sine_rows,
        ],
        axis=-1,
    )


def norm_apply(residual, gain_row, bias_row):
    centre = residual - jnp.mean(residual, axis=-1, keepdims=True)
    spread = jnp.mean(centre * centre, axis=-1, keepdims=True)
    return centre * lax.rsqrt(spread + EPSILON) * gain_row + bias_row


def split_heads(merged, group_count):
    seqs_here, row_count, _ = merged.shape
    return merged.reshape(seqs_here, row_count, group_count, -1, HEAD_DIM).transpose(2, 0, 1, 3, 4)


def join_heads(grouped):
    group_count, seqs_here, row_count, heads_group, head_size = grouped.shape
    return grouped.transpose(1, 2, 0, 3, 4).reshape(
        seqs_here, row_count, group_count * heads_group * head_size
    )


def shards(
    tokens,
    cotangent,
    segments,
    adapter_index,
    qkv_weight,
    out_weight,
    ffn_in_weight,
    ffn_out_weight,
    norm_gain,
    norm_bias,
    adapt_in,
    adapt_down,
    adapt_out,
    adapt_ffn,
):
    seqs_here, tok_rows, model_width = tokens.shape
    heads_group = math.gcd(HEADS, 4)
    group_count = HEADS // heads_group
    score_scale = 1.0 / math.sqrt(HEAD_DIM)
    seq_count = lax.axis_size("seq")
    row_base = lax.axis_index("seq") * tok_rows
    shift_plan = []
    for distance in range(1, min(seq_count, HALF // tok_rows + 2)):
        row_count = min(tok_rows, HALF - (distance - 1) * tok_rows)
        if row_count > 0:
            shift_plan.append((distance, row_count))
            shift_plan.append((-distance, row_count))
    left_total = sum((plan_item[1] for plan_item in shift_plan if plan_item[0] > 0))
    key_rows = 2 * left_total + tok_rows
    key_places = {}
    passed_rows = 0
    for distance, row_count in shift_plan:
        if distance > 0:
            key_places[distance] = left_total - passed_rows - row_count
            key_places[-distance] = left_total + tok_rows + passed_rows
            passed_rows += row_count
    cosine_all, sine_all = rope_tables(segments)
    cosine_here = lax.dynamic_slice_in_dim(cosine_all, row_base, tok_rows, 1)
    sine_here = lax.dynamic_slice_in_dim(sine_all, row_base, tok_rows, 1)
    padded_ids = jnp.pad(segments, ((0, 0), (HALF, HALF)), constant_values=-1)
    key_ids = lax.dynamic_slice_in_dim(padded_ids, row_base - left_total + HALF, key_rows, 1)
    query_ids = lax.dynamic_slice_in_dim(segments, row_base, tok_rows, 1)
    offsets = (
        jnp.arange(tok_rows, dtype=jnp.int32)[:, None]
        - jnp.arange(key_rows, dtype=jnp.int32)[None, :]
        + left_total
    )
    visible = (query_ids[:, :, None] == key_ids[:, None, :]) & (jnp.abs(offsets) <= HALF)[None]
    slot_hits = adapter_index[:, 0][:, None] == jnp.arange(ADAPTERS, dtype=jnp.int32)[None, :]
    slot_low = slot_hits.astype(jnp.bfloat16)
    slot_full = slot_hits.astype(jnp.float32)

    def select_adapter(table):
        return jnp.einsum(
            "se,le...->ls...", slot_low, table, preferred_element_type=jnp.float32
        ).astype(jnp.bfloat16)

    def spread_slots(per_sequence):
        return jnp.einsum("se,s...->e...", slot_full, per_sequence, precision=PRECISE)

    chosen_in = select_adapter(adapt_in)
    chosen_down = select_adapter(adapt_down)
    chosen_out = select_adapter(adapt_out)
    chosen_ffn = select_adapter(adapt_ffn)

    def forward_group(items):
        query_block, key_block, value_block = items
        scores = (
            jnp.einsum(
                "sqhd,skhd->shqk", query_block, key_block, preferred_element_type=jnp.float32
            )
            * score_scale
        )
        scores = jnp.where(visible[:, None], scores, -1e30)
        biggest = jnp.max(scores, axis=-1, keepdims=True)
        lifted = jnp.exp(scores - biggest)
        row_total = jnp.sum(lifted, axis=-1, keepdims=True)
        probability = (lifted / row_total).astype(jnp.bfloat16)
        result = jnp.einsum(
            "shqk,skhd->sqhd", probability, value_block, preferred_element_type=jnp.float32
        )
        return (result.astype(jnp.bfloat16), (biggest + jnp.log(row_total))[..., 0])

    def backward_group(items):
        query_block, key_block, value_block, grad_block, log_total = items
        scores = (
            jnp.einsum(
                "sqhd,skhd->shqk", query_block, key_block, preferred_element_type=jnp.float32
            )
            * score_scale
        )
        scores = jnp.where(visible[:, None], scores, -1e30)
        probability = jnp.exp(scores - log_total[..., None])
        d_prob = jnp.einsum(
            "sqhd,skhd->shqk", grad_block, value_block, preferred_element_type=jnp.float32
        )
        delta = jnp.sum(probability * d_prob, axis=-1, keepdims=True)
        d_score = (probability * (d_prob - delta)).astype(jnp.bfloat16)
        d_query = (
            jnp.einsum("shqk,skhd->sqhd", d_score, key_block, preferred_element_type=jnp.float32)
            * score_scale
        )
        d_key = (
            jnp.einsum("shqk,sqhd->skhd", d_score, query_block, preferred_element_type=jnp.float32)
            * score_scale
        )
        d_value = jnp.einsum(
            "shqk,sqhd->skhd",
            probability.astype(jnp.bfloat16),
            grad_block,
            preferred_element_type=jnp.float32,
        )
        return (d_query, d_key, d_value)

    state = tokens.astype(jnp.float32)
    layer_index = 0
    w_qkv = lax.all_gather(qkv_weight[layer_index], ("batch", "seq"), axis=1, tiled=True)
    w_out = lax.all_gather(out_weight[layer_index], ("batch", "seq"), axis=0, tiled=True)
    w_in = lax.all_gather(ffn_in_weight[layer_index], ("batch", "seq"), axis=1, tiled=True)
    w_down = lax.all_gather(ffn_out_weight[layer_index], ("batch", "seq"), axis=0, tiled=True)
    held = [(w_qkv, w_out, w_in, w_down)]
    act_one = state.astype(jnp.bfloat16)
    low_qkv = jnp.einsum(
        "std,spdr->pstr",
        act_one,
        chosen_in[layer_index][:, 0:3],
        preferred_element_type=jnp.float32,
    ).astype(jnp.bfloat16)
    proj = jnp.einsum(
        "std,pde->pste", act_one, w_qkv, preferred_element_type=jnp.float32
    ) + jnp.einsum(
        "pstr,spre->pste",
        low_qkv,
        chosen_out[layer_index][:, 0:3],
        preferred_element_type=jnp.float32,
    )
    queries = (
        rotate(proj[0].reshape(seqs_here, tok_rows, HEADS, HEAD_DIM), cosine_here, sine_here)
        .astype(jnp.bfloat16)
        .reshape(seqs_here, tok_rows, model_width)
    )
    key_rot = (
        rotate(proj[1].reshape(seqs_here, tok_rows, HEADS, HEAD_DIM), cosine_here, sine_here)
        .astype(jnp.bfloat16)
        .reshape(seqs_here, tok_rows, model_width)
    )
    key_value = jnp.stack([key_rot, proj[2].astype(jnp.bfloat16)])
    edges = {}
    for step_by, row_count in shift_plan:
        if step_by > 0:
            outgoing = key_value[:, :, tok_rows - row_count :]
        else:
            outgoing = key_value[:, :, :row_count]
        edges[step_by] = shifted(outgoing, "seq", step_by)
    earlier = [edges[distance] for distance, row_count in reversed(shift_plan) if distance > 0]
    later = [edges[-distance] for distance, row_count in shift_plan if distance > 0]
    window = jnp.concatenate(earlier + [key_value] + later, axis=2)
    heads_out, log_total = lax.map(
        forward_group,
        (
            split_heads(queries, group_count),
            split_heads(window[0], group_count),
            split_heads(window[1], group_count),
        ),
    )
    attended = join_heads(heads_out)
    low_out = jnp.einsum(
        "std,sdr->str", attended, chosen_in[layer_index][:, 3], preferred_element_type=jnp.float32
    ).astype(jnp.bfloat16)
    branch = jnp.einsum(
        "std,de->ste", attended, w_out, preferred_element_type=jnp.float32
    ) + jnp.einsum(
        "str,sre->ste", low_out, chosen_out[layer_index][:, 3], preferred_element_type=jnp.float32
    )
    resid_one = state + branch
    hidden = norm_apply(resid_one, norm_gain[layer_index, 0], norm_bias[layer_index, 0])
    act_two = hidden.astype(jnp.bfloat16)
    low_ffn = jnp.einsum(
        "std,spdr->pstr",
        act_two,
        chosen_in[layer_index][:, 4:6],
        preferred_element_type=jnp.float32,
    ).astype(jnp.bfloat16)
    gate_up = jnp.einsum(
        "std,pdf->pstf", act_two, w_in, preferred_element_type=jnp.float32
    ) + jnp.einsum(
        "pstr,sprf->pstf", low_ffn, chosen_ffn[layer_index], preferred_element_type=jnp.float32
    )
    inner = (jax.nn.silu(gate_up[0]) * gate_up[1]).astype(jnp.bfloat16)
    low_down = jnp.einsum(
        "stf,sfr->str", inner, chosen_down[layer_index], preferred_element_type=jnp.float32
    ).astype(jnp.bfloat16)
    branch_two = jnp.einsum(
        "stf,fe->ste", inner, w_down, preferred_element_type=jnp.float32
    ) + jnp.einsum(
        "str,sre->ste", low_down, chosen_out[layer_index][:, 4], preferred_element_type=jnp.float32
    )
    resid_two = hidden + branch_two
    kept = [
        (
            act_one,
            low_qkv,
            queries,
            window,
            log_total,
            attended,
            low_out,
            resid_one,
            act_two,
            low_ffn,
            gate_up,
            inner,
            low_down,
            resid_two,
        )
    ]
    state = norm_apply(resid_two, norm_gain[layer_index, 1], norm_bias[layer_index, 1])
    mixed = state.astype(jnp.bfloat16)
    grad = cotangent.astype(jnp.float32)
    collected = [None] * LAYERS
    for layer_index in reversed(range(LAYERS)):
        (
            act_one,
            low_qkv,
            queries,
            window,
            log_total,
            attended,
            low_out,
            resid_one,
            act_two,
            low_ffn,
            gate_up,
            inner,
            low_down,
            resid_two,
        ) = kept[layer_index]
        w_qkv, w_out, w_in, w_down = held[layer_index]
        gain_two = norm_gain[layer_index, 1]
        bias_two = norm_bias[layer_index, 1]
        _, pull_two = jax.vjp(lambda residual: norm_apply(residual, gain_two, bias_two), resid_two)
        (d_resid_two,) = pull_two(grad)
        d_branch_two = d_resid_two.astype(jnp.bfloat16)
        d_low_down = jnp.einsum(
            "ste,sre->str",
            d_branch_two,
            chosen_out[layer_index][:, 4],
            preferred_element_type=jnp.float32,
        ).astype(jnp.bfloat16)
        g_out_down = jnp.einsum(
            "str,ste->sre", low_down, d_branch_two, preferred_element_type=jnp.float32
        )
        g_down = jnp.einsum("stf,str->sfr", inner, d_low_down, preferred_element_type=jnp.float32)
        d_inner = jnp.einsum(
            "ste,fe->stf", d_branch_two, w_down, preferred_element_type=jnp.float32
        ) + jnp.einsum(
            "str,sfr->stf", d_low_down, chosen_down[layer_index], preferred_element_type=jnp.float32
        )
        _, pull_act = jax.vjp(
            lambda gate_part, up_part: jax.nn.silu(gate_part) * up_part, gate_up[0], gate_up[1]
        )
        d_gate, d_up = pull_act(d_inner)
        d_gate_up = jnp.stack([d_gate, d_up]).astype(jnp.bfloat16)
        d_low_ffn = jnp.einsum(
            "pstf,sprf->pstr",
            d_gate_up,
            chosen_ffn[layer_index],
            preferred_element_type=jnp.float32,
        ).astype(jnp.bfloat16)
        g_ffn = jnp.einsum(
            "pstr,pstf->sprf", low_ffn, d_gate_up, preferred_element_type=jnp.float32
        )
        g_in_ffn = jnp.einsum(
            "std,pstr->spdr", act_two, d_low_ffn, preferred_element_type=jnp.float32
        )
        ffn_in_sum = spread_slots(g_in_ffn)
        ffn_down_sum = spread_slots(g_down)
        ffn_out_sum = spread_slots(g_out_down[:, None])
        ffn_ffn_sum = spread_slots(g_ffn)
        d_hidden = (
            d_resid_two
            + jnp.einsum("pstf,pdf->std", d_gate_up, w_in, preferred_element_type=jnp.float32)
            + jnp.einsum(
                "pstr,spdr->std",
                d_low_ffn,
                chosen_in[layer_index][:, 4:6],
                preferred_element_type=jnp.float32,
            )
        )
        gain_one = norm_gain[layer_index, 0]
        bias_one = norm_bias[layer_index, 0]
        _, pull_one = jax.vjp(lambda residual: norm_apply(residual, gain_one, bias_one), resid_one)
        (d_resid_one,) = pull_one(d_hidden)
        d_branch = d_resid_one.astype(jnp.bfloat16)
        d_low_out = jnp.einsum(
            "ste,sre->str",
            d_branch,
            chosen_out[layer_index][:, 3],
            preferred_element_type=jnp.float32,
        ).astype(jnp.bfloat16)
        g_out_att = jnp.einsum(
            "str,ste->sre", low_out, d_branch, preferred_element_type=jnp.float32
        )
        g_in_att = jnp.einsum(
            "std,str->sdr", attended, d_low_out, preferred_element_type=jnp.float32
        )
        d_attended = (
            jnp.einsum("ste,de->std", d_branch, w_out, preferred_element_type=jnp.float32)
            + jnp.einsum(
                "str,sdr->std",
                d_low_out,
                chosen_in[layer_index][:, 3],
                preferred_element_type=jnp.float32,
            )
        ).astype(jnp.bfloat16)
        d_query_heads, d_key_heads, d_value_heads = lax.map(
            backward_group,
            (
                split_heads(queries, group_count),
                split_heads(window[0], group_count),
                split_heads(window[1], group_count),
                split_heads(d_attended, group_count),
                log_total,
            ),
        )
        d_query = join_heads(d_query_heads)
        d_window = jnp.stack([join_heads(d_key_heads), join_heads(d_value_heads)])
        d_pair = d_window[:, :, left_total : left_total + tok_rows]
        for step_by, row_count in shift_plan:
            returning = lax.slice_in_dim(
                d_window, key_places[step_by], key_places[step_by] + row_count, axis=2
            )
            arrived = shifted(returning.astype(jnp.bfloat16), "seq", -step_by).astype(
                returning.dtype
            )
            if step_by > 0:
                d_pair = d_pair.at[:, :, tok_rows - row_count :].add(arrived)
            else:
                d_pair = d_pair.at[:, :, :row_count].add(arrived)
        d_query_rot = rotate(
            d_query.reshape(seqs_here, tok_rows, HEADS, HEAD_DIM), cosine_here, -sine_here
        ).reshape(seqs_here, tok_rows, model_width)
        d_key_rot = rotate(
            d_pair[0].reshape(seqs_here, tok_rows, HEADS, HEAD_DIM), cosine_here, -sine_here
        ).reshape(seqs_here, tok_rows, model_width)
        d_proj = jnp.stack([d_query_rot, d_key_rot, d_pair[1]]).astype(jnp.bfloat16)
        d_low_qkv = jnp.einsum(
            "pste,spre->pstr",
            d_proj,
            chosen_out[layer_index][:, 0:3],
            preferred_element_type=jnp.float32,
        ).astype(jnp.bfloat16)
        g_out_qkv = jnp.einsum(
            "pstr,pste->spre", low_qkv, d_proj, preferred_element_type=jnp.float32
        )
        g_in_qkv = jnp.einsum(
            "std,pstr->spdr", act_one, d_low_qkv, preferred_element_type=jnp.float32
        )
        grad = (
            d_resid_one
            + jnp.einsum("pste,pde->std", d_proj, w_qkv, preferred_element_type=jnp.float32)
            + jnp.einsum(
                "pstr,spdr->std",
                d_low_qkv,
                chosen_in[layer_index][:, 0:3],
                preferred_element_type=jnp.float32,
            )
        )
        att_in_sum = spread_slots(jnp.concatenate([g_in_qkv, g_in_att[:, None]], axis=1))
        att_out_sum = spread_slots(jnp.concatenate([g_out_qkv, g_out_att[:, None]], axis=1))
        collected[layer_index] = (
            jnp.concatenate([att_in_sum, ffn_in_sum], axis=1),
            ffn_down_sum,
            jnp.concatenate([att_out_sum, ffn_out_sum], axis=1),
            ffn_ffn_sum,
        )
    input_grad = grad.astype(jnp.bfloat16)
    stack_in = jnp.stack([collected[0][0]])
    stack_down = jnp.stack([collected[0][1]])
    stack_out = jnp.stack([collected[0][2]])
    stack_ffn = jnp.stack([collected[0][3]])
    stack_in, stack_down, stack_out, stack_ffn = lax.psum(
        (stack_in, stack_down, stack_out, stack_ffn), ("batch", "seq")
    )
    return (mixed, input_grad, stack_in, stack_down, stack_out, stack_ffn)


def solution(mesh):
    return jax.shard_map(
        shards,
        mesh=mesh,
        in_specs=(
            P("batch", "seq", None),
            P("batch", "seq", None),
            P("batch", None),
            P("batch", None),
            P(None, None, ("batch", "seq"), None),
            P(None, ("batch", "seq"), None),
            P(None, None, ("batch", "seq"), None),
            P(None, ("batch", "seq"), None),
            P(),
            P(),
            P(),
            P(),
            P(),
            P(),
        ),
        out_specs=(P("batch", "seq", None), P("batch", "seq", None), P(), P(), P(), P()),
        check_vma=False,
    )
```

profile of v0, /device:TPU:1, one launch (start us, length us, event | category | flops | bytes accessed | tf_op | source)
XLA Modules:
  0.0 1005.3 jit_solution(12956359871055918713)
XLA Ops:
  21.8 52.0 %all-gather.9.cloned.1.call-done = bf16[1,3,768,768]{3,2,1,0:T(8,128)(2,1)} async-done(((bf16[1,3,24,768]{3,2,1,0:T(8,128)(2,1)}), bf16[1,3,768,768]{3,2,1,0:T(8,128)(2,1)}) %all-gather.9.cloned.1.call-update) | async-done | bytes 3538960 | tf_op jit(solution)/shard_map/all_gather | solution.py:196
  137.5 154.6 %while.30 = (s32[]{:T(128)}, bf16[3,1,1024,4,64]{2,4,3,1,0:T(8,128)(2,1)}, f32[3,1,4,1024]{3,2,1,0:T(4,128)}, bf16[3,1,2048,4,64]{2,4,3,1,0:T(8,128)(2,1)}, bf16...) while((s32[]{:T(128)}, ...), condition=%wide.region_5.6_spmd.clone, body=%wide.region_2.5_spmd.clone.sunk | while | flops 2260987904 | bytes 112343136 | solution.py:237
  141.6 15.3 %fusion.210 = (f32[4,1024]{1,0:T(4,128)S(1)}, f32[4,1024,2048]{2,1,0:T(8,128)}) fusion(pred[1024,2048]{1,0:T(8,128)(4,1)S(1)} %fusion.209, bf16[3,1,2048,4,64]{2,4,3,1,0:T(8,128)(2,1)} %get-tuple-element.435, s32[]{:T(128)S(6)} %copy.160, bf16[3,1,1024,4,64]{2,4,3,1,0:T(8,128)(2,1)S(1)} %get-tuple-element.434), kind=kOutput, calls=%fused_computation.5.clone.1 | convolution fusion | flops 1098903552 | bytes 37241856 | tf_op jit(solution)/shard_map/while/body/eval_jaxpr/sqhd,skhd->shqk/dot_general | solution.py:148
  156.9 15.1 %fusion.211 = f32[4,1024]{1,0:T(4,128)S(1)} fusion(f32[4,1024,2048]{2,1,0:T(8,128)} %get-tuple-element.397, f32[4,1024]{1,0:T(4,128)S(1)} %get-tuple-element.398, pred[1024,2048]{1,0:T(8,128)(4,1)S(1)} %fusion.209), kind=kLoop, calls=%fused_computation.6.clone.1 | loop fusion | flops 33550336 | bytes 35684352 | tf_op jit(solution)/shard_map/while/body/eval_jaxpr/reduce_sum | solution.py:156
  172.0 16.6 %fusion.212 = bf16[3,1,1024,4,64]{2,4,3,1,0:T(8,128)(2,1)} fusion(bf16[3,1,1024,4,64]{2,4,3,1,0:T(8,128)(2,1)} %get-tuple-element.422, s32[]{:T(128)S(6)} %copy.160, f32[4,1024,2048]{2,1,0:T(8,128)} %get-tuple-element.397, f32[4,1024]{1,0:T(4,128)S(1)} %fusion.211, f32[4,1024]{1,0:T(4,128)S(1)} %get-tuple-element.398, ...), kind=kOutput, calls=%fused_computation.13.clone.1 | convolution fusion | flops 1115947008 | bytes 37258240 | tf_op jit(solution)/shard_map/while/body/eval_jaxpr/shqk,skhd->sqhd/dot_general | solution.py:158
  193.4 15.8 %fusion.210 = (f32[4,1024]{1,0:T(4,128)S(1)}, f32[4,1024,2048]{2,1,0:T(8,128)}) fusion(pred[1024,2048]{1,0:T(8,128)(4,1)S(1)} %fusion.209, bf16[3,1,2048,4,64]{2,4,3,1,0:T(8,128)(2,1)} %get-tuple-element.435, s32[]{:T(128)S(6)} %copy.160, bf16[3,1,1024,4,64]{2,4,3,1,0:T(8,128)(2,1)S(1)} %get-tuple-element.434), kind=kOutput, calls=%fused_computation.5.clone.1 | convolution fusion | flops 1098903552 | bytes 37241856 | tf_op jit(solution)/shard_map/while/body/eval_jaxpr/sqhd,skhd->shqk/dot_general | solution.py:148
  209.2 15.2 %fusion.211 = f32[4,1024]{1,0:T(4,128)S(1)} fusion(f32[4,1024,2048]{2,1,0:T(8,128)} %get-tuple-element.397, f32[4,1024]{1,0:T(4,128)S(1)} %get-tuple-element.398, pred[1024,2048]{1,0:T(8,128)(4,1)S(1)} %fusion.209), kind=kLoop, calls=%fused_computation.6.clone.1 | loop fusion | flops 33550336 | bytes 35684352 | tf_op jit(solution)/shard_map/while/body/eval_jaxpr/reduce_sum | solution.py:156
  224.4 15.4 %fusion.212 = bf16[3,1,1024,4,64]{2,4,3,1,0:T(8,128)(2,1)} fusion(bf16[3,1,1024,4,64]{2,4,3,1,0:T(8,128)(2,1)} %get-tuple-element.422, s32[]{:T(128)S(6)} %copy.160, f32[4,1024,2048]{2,1,0:T(8,128)} %get-tuple-element.397, f32[4,1024]{1,0:T(4,128)S(1)} %fusion.211, f32[4,1024]{1,0:T(4,128)S(1)} %get-tuple-element.398, ...), kind=kOutput, calls=%fused_computation.13.clone.1 | convolution fusion | flops 1115947008 | bytes 37258240 | tf_op jit(solution)/shard_map/while/body/eval_jaxpr/shqk,skhd->sqhd/dot_general | solution.py:158
  244.5 15.3 %fusion.210 = (f32[4,1024]{1,0:T(4,128)S(1)}, f32[4,1024,2048]{2,1,0:T(8,128)}) fusion(pred[1024,2048]{1,0:T(8,128)(4,1)S(1)} %fusion.209, bf16[3,1,2048,4,64]{2,4,3,1,0:T(8,128)(2,1)} %get-tuple-element.435, s32[]{:T(128)S(6)} %copy.160, bf16[3,1,1024,4,64]{2,4,3,1,0:T(8,128)(2,1)S(1)} %get-tuple-element.434), kind=kOutput, calls=%fused_computation.5.clone.1 | convolution fusion | flops 1098903552 | bytes 37241856 | tf_op jit(solution)/shard_map/while/body/eval_jaxpr/sqhd,skhd->shqk/dot_general | solution.py:148
  259.8 15.7 %fusion.211 = f32[4,1024]{1,0:T(4,128)S(1)} fusion(f32[4,1024,2048]{2,1,0:T(8,128)} %get-tuple-element.397, f32[4,1024]{1,0:T(4,128)S(1)} %get-tuple-element.398, pred[1024,2048]{1,0:T(8,128)(4,1)S(1)} %fusion.209), kind=kLoop, calls=%fused_computation.6.clone.1 | loop fusion | flops 33550336 | bytes 35684352 | tf_op jit(solution)/shard_map/while/body/eval_jaxpr/reduce_sum | solution.py:156
  275.5 15.5 %fusion.212 = bf16[3,1,1024,4,64]{2,4,3,1,0:T(8,128)(2,1)} fusion(bf16[3,1,1024,4,64]{2,4,3,1,0:T(8,128)(2,1)} %get-tuple-element.422, s32[]{:T(128)S(6)} %copy.160, f32[4,1024,2048]{2,1,0:T(8,128)} %get-tuple-element.397, f32[4,1024]{1,0:T(4,128)S(1)} %fusion.211, f32[4,1024]{1,0:T(4,128)S(1)} %get-tuple-element.398, ...), kind=kOutput, calls=%fused_computation.13.clone.1 | convolution fusion | flops 1115947008 | bytes 37258240 | tf_op jit(solution)/shard_map/while/body/eval_jaxpr/shqk,skhd->sqhd/dot_general | solution.py:158
  300.6 17.3 %fusion.67 = f32[1024,2,3072]{2,0,1:T(8,128)} fusion(bf16[1024,768,1]{0,1,2:T(8,128)(2,1)S(1)} %fusion.96, bf16[1,2,768,3072]{3,2,1,0:T(8,128)(2,1)} %all-gather.13.cloned.1.call-done), kind=kOutput, calls=%fused_computation.89 | convolution fusion | flops 9663676416 | bytes 36175872 | tf_op jit(solution)/shard_map/std,pdf->pstf/dot_general | solution.py:263
  317.8 16.4 %bitcast_add_fusion = f32[2,1,1024,3072]{3,2,0,1:T(8,128)} fusion(f32[1024,2,3072]{2,0,1:T(8,128)} %fusion.67, bf16[2,1024,16]{1,2,0:T(8,128)(2,1)S(1)} %fusion.120, bf16[1,2,16,3072]{3,0,2,1:T(2,128)(2,1)S(1)} %copy-done.56), kind=kOutput, calls=%fused_computation.63 | convolution fusion | flops 207618048 | bytes 50593792 | tf_op jit(solution)/shard_map/pstr,sprf->pstf/dot_general | solution.py:265
  379.6 19.6 %fusion.77 = (bf16[1,1024,3072]{2,1,0:T(8,128)(2,1)}, bf16[1,1024,3072]{2,1,0:T(8,128)(2,1)}) fusion(f32[2,1,1024,3072]{3,2,0,1:T(8,128)} %bitcast_add_fusion, f32[1024,3072]{1,0:T(8,128)} %fusion.78, bf16[1024,16]{0,1:T(8,128)(2,1)S(1)} %convolution_convert_fusion.3, bf16[1,3072,16]{1,2,0:T(8,128)(2,1)S(1)} %copy-done.46), kind=kOutput, calls=%fused_computation.100 | convolution fusion | flops 147849216 | bytes 50462720 | tf_op jit(solution)/shard_map/str,sfr->stf/dot_general | solution.py:335
  407.0 15.8 %fusion.65 = f32[1024,768,1]{0,1,2:T(8,128)S(1)} fusion(bf16[1,2,768,3072]{3,2,1,0:T(8,128)(2,1)} %all-gather.13.cloned.1.call-done, bf16[1,1024,3072]{2,1,0:T(8,128)(2,1)} %get-tuple-element.252, bf16[1,1024,3072]{2,1,0:T(8,128)(2,1)} %get-tuple-element.251), kind=kOutput, calls=%fused_computation.87 | convolution fusion | flops 9669967872 | bytes 25165824 | tf_op jit(solution)/shard_map/pstf,pdf->std/dot_general | solution.py:361
  432.8 329.1 %while.31 = (s32[]{:T(128)}, f32[3,1,1024,4,64]{2,4,3,1,0:T(8,128)}, f32[3,1,2048,4,64]{2,4,3,1,0:T(8,128)}, f32[3,1,2048,4,64]{2,4,3,1,0:T(8,128)}, bf16[3,1,20...) while((s32[]{:T(128)}, ...), condition=%wide.region_16.17_spmd.clone, body=%wide.region_14.16_spmd.clone.sunk | while | flops 5457571840 | bytes 266437776 | solution.py:395
  452.2 25.3 %multiply_reduce_fusion.6 = (f32[4,1024]{1,0:T(4,128)S(1)}, f32[4,1024,2048]{2,1,0:T(8,128)}) fusion(f32[4,1024,2048]{2,1,0:T(8,128)} %fusion.221, f32[4,1024]{1,0:T(4,128)S(1)} %dynamic-slice_bitcast_fusion.2, bf16[3,1,2048,4,64]{2,4,3,1,0:T(8,128)(2,1)} %get-tuple-element.467, s32[]{:T(128)S(6)} %copy.170, ...), kind=kOutput, calls=%fused_computation.27.clone.1 | convolution fusion | flops 1115680768 | bytes 70812672 | tf_op jit(solution)/shard_map/while/body/eval_jaxpr/sqhd,skhd->shqk/dot_general | solution.py:166
  477.6 27.4 %multiply_convert_fusion.4 = bf16[4,1024,2048]{2,1,0:T(8,128)(2,1)} fusion(f32[4,1024,2048]{2,1,0:T(8,128)} %get-tuple-element.410, f32[4,1024,2048]{2,1,0:T(8,128)} %fusion.221, f32[4,1024]{1,0:T(4,128)S(1)} %get-tuple-element.411), kind=kLoop, calls=%fused_computation.26.clone.1 | loop fusion | flops 25165824 | bytes 83902464 | tf_op jit(solution)/shard_map/while/body/eval_jaxpr/convert_element_type | solution.py:177
  561.8 25.4 %multiply_reduce_fusion.6 = (f32[4,1024]{1,0:T(4,128)S(1)}, f32[4,1024,2048]{2,1,0:T(8,128)}) fusion(f32[4,1024,2048]{2,1,0:T(8,128)} %fusion.221, f32[4,1024]{1,0:T(4,128)S(1)} %dynamic-slice_bitcast_fusion.2, bf16[3,1,2048,4,64]{2,4,3,1,0:T(8,128)(2,1)} %get-tuple-element.467, s32[]{:T(128)S(6)} %copy.170, ...), kind=kOutput, calls=%fused_computation.27.clone.1 | convolution fusion | flops 1115680768 | bytes 70812672 | tf_op jit(solution)/shard_map/while/body/eval_jaxpr/sqhd,skhd->shqk/dot_general | solution.py:166
  587.2 27.4 %multiply_convert_fusion.4 = bf16[4,1024,2048]{2,1,0:T(8,128)(2,1)} fusion(f32[4,1024,2048]{2,1,0:T(8,128)} %get-tuple-element.410, f32[4,1024,2048]{2,1,0:T(8,128)} %fusion.221, f32[4,1024]{1,0:T(4,128)S(1)} %get-tuple-element.411), kind=kLoop, calls=%fused_computation.26.clone.1 | loop fusion | flops 25165824 | bytes 83902464 | tf_op jit(solution)/shard_map/while/body/eval_jaxpr/convert_element_type | solution.py:177
  671.3 25.3 %multiply_reduce_fusion.6 = (f32[4,1024]{1,0:T(4,128)S(1)}, f32[4,1024,2048]{2,1,0:T(8,128)}) fusion(f32[4,1024,2048]{2,1,0:T(8,128)} %fusion.221, f32[4,1024]{1,0:T(4,128)S(1)} %dynamic-slice_bitcast_fusion.2, bf16[3,1,2048,4,64]{2,4,3,1,0:T(8,128)(2,1)} %get-tuple-element.467, s32[]{:T(128)S(6)} %copy.170, ...), kind=kOutput, calls=%fused_computation.27.clone.1 | convolution fusion | flops 1115680768 | bytes 70812672 | tf_op jit(solution)/shard_map/while/body/eval_jaxpr/sqhd,skhd->shqk/dot_general | solution.py:166
  696.7 27.4 %multiply_convert_fusion.4 = bf16[4,1024,2048]{2,1,0:T(8,128)(2,1)} fusion(f32[4,1024,2048]{2,1,0:T(8,128)} %get-tuple-element.410, f32[4,1024,2048]{2,1,0:T(8,128)} %fusion.221, f32[4,1024]{1,0:T(4,128)S(1)} %get-tuple-element.411), kind=kLoop, calls=%fused_computation.26.clone.1 | loop fusion | flops 25165824 | bytes 83902464 | tf_op jit(solution)/shard_map/while/body/eval_jaxpr/convert_element_type | solution.py:177
  798.0 26.1 %collective-permute-done.2 = bf16[2,1,512,768]{3,2,1,0:T(8,128)(2,1)S(1)} collective-permute-done((bf16[2,1,512,768]{3,2,1,0:T(8,128)(2,1)S(1)}, bf16[2,1,512,768]{3,2,1,0:T(8,128)(2,1)S(1)}, u32[]{:S(2)}, u32[]{:S(2)}) %collective-permute-start.2) | collective-permute-done | bytes 1572896 | tf_op jit(solution)/shard_map/ppermute | solution.py:23
  862.8 128.9 %all-reduce.4.cloned.1.call-done = (f32[1,4,6,768,16]{3,4,2,1,0:T(8,128)}, f32[1,4,3072,16]{2,3,1,0:T(8,128)}, f32[1,4,5,16,768]{4,3,2,1,0:T(8,128)}, f32[1,4,2,16,3072]{4,3,2,1,0:T(8,128)}) async-done(((f32[1,4,6,768,16]{3,4,2,1,0:T(8,128)}, f32[1,4,3072,16]{2,3,1,0:T(8,128)}, f32[1,4,5,16,768]{4,3,2,1,0:T(8,128)}, f32[1,4,2,16,3072]{4,3,2,1,0:T(8,128)}), (f32[1,4,6,768,16]{3,4,2,1,0:T(8,128)}, ...) | async-done | bytes 4522000 | tf_op jit(solution)/shard_map/psum | solution.py:461
  (317 shorter events, 414.3 us)
Async XLA Ops:
  7.2 106.1 %copy-start = (bf16[1,4,2,16,3072]{4,3,2,1,0:T(8,128)(2,1)S(1)}, bf16[1,4,2,16,3072]{4,3,2,1,0:T(8,128)(2,1)}, u32[]{:S(2)}) copy-start(bf16[1,4,2,16,3072]{4,3,2,1,0:T(8,128)(2,1)} %param.35) | copy-start | bytes 2359300
  7.2 66.5 %all-gather.9.cloned.1.call-start = ((), (), s32[]{:S(2)}) async-start(), calls=%async_computation | async-start | bytes 3649536 | tf_op jit(solution)/shard_map/all_gather | solution.py:196
  7.9 286.5 %all-gather.11.cloned.1.call-start = ((), (), s32[]{:S(2)}) async-start(), calls=%async_computation.1 | async-start | bytes 1216512 | tf_op jit(solution)/shard_map/all_gather | solution.py:197
  8.7 291.9 %all-gather.13.cloned.1.call-start = ((), (), s32[]{:S(2)}) async-start(), calls=%async_computation.2 | async-start | bytes 9732096 | tf_op jit(solution)/shard_map/all_gather | solution.py:198
  9.4 339.1 %all-gather.15.cloned.1.call-start = ((), (), s32[]{:S(2)}) async-start(), calls=%async_computation.3 | async-start | bytes 4866048 | tf_op jit(solution)/shard_map/all_gather | solution.py:199
  10.0 981.7 %all-reduce.4.cloned.1.call-start = ((), (), s32[]{:S(2)}) async-start(), calls=%async_computation.4 | async-start | bytes 9043968 | tf_op jit(solution)/shard_map/psum | solution.py:461
  14.0 65.9 %copy-start.37 = (bf16[1,5,16,768]{3,2,1,0:T(8,128)(2,1)}, bf16[1,5,16,768]{3,2,1,0:T(8,128)(2,1)S(1)}, u32[]{:S(2)}) copy-start(bf16[1,5,16,768]{3,2,1,0:T(8,128)(2,1)S(1)} %copy.151) | copy-start | bytes 368644
  17.9 61.9 %copy-start.44 = (bf16[3,1024,16]{1,2,0:T(8,128)(2,1)}, bf16[3,1024,16]{1,2,0:T(8,128)(2,1)S(1)}, u32[]{:S(2)}) copy-start(bf16[3,1024,16]{1,2,0:T(8,128)(2,1)S(1)} %fusion.116) | copy-start | bytes 294916
  21.8 60.9 %copy-start.31 = (f32[1024,32]{0,1:T(8,128)}, f32[1024,32]{0,1:T(8,128)S(1)}, u32[]{:S(2)}) copy-start(f32[1024,32]{0,1:T(8,128)S(1)} %get-tuple-element.275) | copy-start | bytes 393220
  87.0 39.6 %collective-permute-start = (bf16[2,1,512,768]{2,3,0,1:T(8,128)(2,1)}, bf16[2,1,512,768]{2,3,0,1:T(8,128)(2,1)}, u32[]{:S(2)}, u32[]{:S(2)}) collective-permute-start(bf16[2,1,512,768]{2,3,0,1:T(8,128)(2,1)} %get-tuple-element.269), channel_id=1, source_target_pairs={{0,1},{2,3},{4,5},{6,7},{8,9},{10,11},{12,13},{14,15},{16,17},{18,... | collective-permute-start | bytes 4718600 | tf_op jit(solution)/shard_map/ppermute | solution.py:23
  91.2 40.3 %collective-permute-start.1 = (bf16[2,1,512,768]{2,3,0,1:T(8,128)(2,1)}, bf16[2,1,512,768]{2,3,0,1:T(8,128)(2,1)}, u32[]{:S(2)}, u32[]{:S(2)}) collective-permute-start(bf16[2,1,512,768]{2,3,0,1:T(8,128)(2,1)} %get-tuple-element.270), channel_id=1, source_target_pairs={{1,0},{3,2},{5,4},{7,6},{9,8},{11,10},{13,12},{15,14},{17,16},{19,... | collective-permute-start | bytes 4718600 | tf_op jit(solution)/shard_map/ppermute | solution.py:23
  110.8 20.6 %copy-start.16 = (bf16[1,1,1024,768]{2,3,0,1:T(8,128)(2,1)S(1)}, bf16[1,1,1024,768]{2,3,0,1:T(8,128)(2,1)}, u32[]{:S(2)}) copy-start(bf16[1,1,1024,768]{2,3,0,1:T(8,128)(2,1)} %copy-done.15) | copy-start | bytes 4718596
  110.8 20.6 %copy-start.18 = (bf16[1,1024,12,64]{1,3,2,0:T(8,128)(2,1)S(1)}, bf16[1,1024,12,64]{1,3,2,0:T(8,128)(2,1)}, u32[]{:S(2)}) copy-start(bf16[1,1024,12,64]{1,3,2,0:T(8,128)(2,1)} %copy-done.17) | copy-start | bytes 4718596
  137.5 154.6 %copy-start.29 = (bf16[1,6,768,16]{2,3,1,0:T(8,128)(2,1)S(1)}, bf16[1,6,768,16]{2,3,1,0:T(8,128)(2,1)}, u32[]{:S(2)}) copy-start(bf16[1,6,768,16]{2,3,1,0:T(8,128)(2,1)} %copy-done.28) | copy-start | bytes 442372
  300.1 17.7 %copy-start.13 = (bf16[1024,768,1]{0,1,2:T(8,128)(2,1)}, bf16[1024,768,1]{0,1,2:T(8,128)(2,1)S(1)}, u32[]{:S(2)}) copy-start(bf16[1024,768,1]{0,1,2:T(8,128)(2,1)S(1)} %fusion.96) | copy-start | bytes 4718596
  300.5 17.3 %copy-start.50 = (bf16[2,1024,16]{1,2,0:T(8,128)(2,1)}, bf16[2,1024,16]{1,2,0:T(8,128)(2,1)S(1)}, u32[]{:S(2)}) copy-start(bf16[2,1024,16]{1,2,0:T(8,128)(2,1)S(1)} %fusion.120) | copy-start | bytes 196612
  300.5 17.3 %copy-start.56 = (bf16[1,2,16,3072]{3,0,2,1:T(2,128)(2,1)S(1)}, bf16[1,2,16,3072]{3,0,2,1:T(2,128)(2,1)}, u32[]{:S(2)}) copy-start(bf16[1,2,16,3072]{3,0,2,1:T(2,128)(2,1)} %fusion.124) | copy-start | bytes 589828
  348.6 13.8 %copy-start.3 = (f32[1,1024,768]{1,2,0:T(8,128)S(1)}, f32[1,1024,768]{1,2,0:T(8,128)}, u32[]{:S(2)}) copy-start(f32[1,1024,768]{1,2,0:T(8,128)} %copy-done.2) | copy-start | bytes 9437188
  407.0 15.9 %copy-start.4 = (f32[1,1024,768]{1,2,0:T(8,128)S(1)}, f32[1,1024,768]{1,2,0:T(8,128)}, u32[]{:S(2)}) copy-start(f32[1,1024,768]{1,2,0:T(8,128)} %copy-done.2) | copy-start | bytes 9437188
  407.0 15.9 %copy-start.7 = (f32[1,1024,768]{1,2,0:T(8,128)S(1)}, f32[1,1024,768]{1,2,0:T(8,128)}, u32[]{:S(2)}) copy-start(f32[1,1024,768]{1,2,0:T(8,128)} %copy-done.6) | copy-start | bytes 9437188
  785.7 38.7 %collective-permute-start.3 = (bf16[2,1,512,768]{3,2,1,0:T(8,128)(2,1)S(1)}, bf16[2,1,512,768]{3,2,1,0:T(8,128)(2,1)S(1)}, u32[]{:S(2)}, u32[]{:S(2)}) collective-permute-start(bf16[2,1,512,768]{3,2,1,0:T(8,128)(2,1)S(1)} %get-tuple-element.255), channel_id=1, source_target_pairs={{0,1},{2,3},{4,5},{6,7},{8,9},{10,11},{12,13},{14,15},{16,17},{18,... | collective-permute-start | bytes 4718600 | tf_op jit(solution)/shard_map/ppermute | solution.py:23
  787.4 36.7 %collective-permute-start.2 = (bf16[2,1,512,768]{3,2,1,0:T(8,128)(2,1)S(1)}, bf16[2,1,512,768]{3,2,1,0:T(8,128)(2,1)S(1)}, u32[]{:S(2)}, u32[]{:S(2)}) collective-permute-start(bf16[2,1,512,768]{3,2,1,0:T(8,128)(2,1)S(1)} %get-tuple-element.256), channel_id=1, source_target_pairs={{1,0},{3,2},{5,4},{7,6},{9,8},{11,10},{13,12},{15,14},{17,16},{19,... | collective-permute-start | bytes 4718600 | tf_op jit(solution)/shard_map/ppermute | solution.py:23
  789.0 35.1 %slice-start = ((s8[6291456]{0:T(1024)(128)(4,1)}), s8[2097152]{0:T(1024)(128)(4,1)S(1)}, s32[]{:S(2)}) async-start(s8[6291456]{0:T(1024)(128)(4,1)} %bitcast.472), calls=%async_computation.5 | async-start | bytes 4194304
  791.7 32.3 %slice-start.1 = ((s8[6291456]{0:T(1024)(128)(4,1)}), s8[4194304]{0:T(1024)(128)(4,1)S(1)}, s32[]{:S(2)}) async-start(s8[6291456]{0:T(1024)(128)(4,1)} %bitcast.472), calls=%async_computation.6 | async-start | bytes 8388608
  (63 other events, 255.4 us)
Sparse Core Ops, SparseCore 0:
  11.0 62.6 all-gather.8
  76.6 54.3 all-gather.10
  134.0 81.2 all-gather.12
  218.1 62.2 all-gather.14
  849.7 141.9 all-reduce.3
where the time goes:
time: 1020 us; the launch traced here: 1010 us
  matrix products  482 us (47%)
  waiting for transfers between devices  225 us (22%)
  other arithmetic  206 us (20%)
  local copies, waits for them, and re-layouts  66.5 us (7%)
  between operations  15.9 us (2%)
    psum x1, waiting for transfers between devices, shards(): lax.psum((stack_in, stack_down, stack_out, stack_ffn), ('batch', 'seq'))  129 us
    convert_element_type x3, other arithmetic, backward_group(): d_score = (probability * (d_prob - delta)).astype(jnp.bfloat16)  82.3 us
    dot_general x3, matrix products, backward_group(): jnp.einsum('sqhd,skhd->shqk', query_block, key_block, preferred_element_t...  76.1 us
    all_gather x1, waiting for transfers between devices, shards(): lax.all_gather(qkv_weight[layer_index], ('batch', 'seq'), axis=1, tiled=T...  52 us
    dot_general x3, matrix products, forward_group(): jnp.einsum('shqk,skhd->sqhd', probability, value_block, preferred_element...  47.5 us
    dot_general x3, matrix products, forward_group(): jnp.einsum('sqhd,skhd->shqk', query_block, key_block, preferred_element_t...  46.4 us
    reduce_sum x3, other arithmetic, forward_group(): row_total = jnp.sum(lifted, axis=-1, keepdims=True)  46 us
    dot_general x3, matrix products, backward_group(): jnp.einsum('shqk,sqhd->skhd', probability.astype(jnp.bfloat16), grad_bloc...  44.9 us
  transfers between devices with their start and end apart: 9, of which 5 were waited for; matrix products, arithmetic and copies ran while one was open for 28% of the time, Pallas kernels for 0%

commit v1 on v0

--- a/solution.py
+++ b/solution.py
@@ -1,8 +1,11 @@
+import functools
 import math
 
 import jax
 import jax.numpy as jnp
 from jax import lax
+from jax.experimental import pallas as pl
+from jax.experimental.pallas import tpu as pltpu
 from jax.sharding import PartitionSpec as P
 
 HEADS = 12
@@ -10,6 +13,8 @@
 ADAPTERS = 4
 LAYERS = 1
 HALF = 512
+D = HEADS * HEAD_DIM
+FF = 4 * D
 
 
 EPSILON = 1e-06
@@ -464,9 +469,807 @@
     return (mixed, input_grad, stack_in, stack_down, stack_out, stack_ffn)
 
 
+BF = jnp.bfloat16
+F32 = jnp.float32
+QB = 256
+PLAN = ((0, 3, False, True), (0, 4, False, True), (0, 5, True, True), (1, 5, True, True))
+HALO_PLAN = ((2, 2), (3, 1))
+NEG = -1e30
+VMEM_LIMIT = int(63.9 * 2**20)
+
+
+def nn(a, b):
+    return jnp.dot(a, b, preferred_element_type=F32)
+
+
+def nt(a, b):
+    return lax.dot_general(a, b, (((1,), (1,)), ((), ())), preferred_element_type=F32)
+
+
+def tn(a, b):
+    return lax.dot_general(a, b, (((0,), (0,)), ((), ())), preferred_element_type=F32)
+
+
+def iota(shape, dim):
+    return lax.broadcasted_iota(jnp.int32, shape, dim)
+
+
+def block_at(flip, block):
+    return pl.multiple_of(jnp.where(flip == 1, 3 - block, block) * QB, QB)
+
+
+def rope(vectors, cosine, sine):
+    lane = iota((1, 128), 1)
+    first = lax.rem(lane, HEAD_DIM) < HEAD_DIM // 2
+    out = []
+    for c in range(vectors.shape[1] // 128):
+        part = vectors[:, c * 128 : (c + 1) * 128]
+        other = jnp.where(first, pltpu.roll(part, 96, 1), pltpu.roll(part, 32, 1))
+        out.append(part * cosine + other * sine)
+    return jnp.concatenate(out, axis=1)
+
+
+def fill_tables(flip, seg_ref, freq_ref, cos_ref, sin_ref, fq_ref, fk_ref, bias_ref):
+    lane = iota((1, 128), 1)
+    seg_row = seg_ref[...].astype(F32)
+    starts = [
+        jnp.sum((seg_row < float(d)).astype(F32), axis=1, keepdims=True) for d in (1, 2, 3)
+    ]
+    sign = jnp.where(lax.rem(lane, HEAD_DIM) < HEAD_DIM // 2, -1.0, 1.0)
+    for w in range(12):
+        block, part = divmod(w, 2)
+        base = jnp.where(flip == 1, 7 - block, block) * QB + part * 128
+        row = seg_ref[:, pl.ds(pl.multiple_of(base, 128), 128)].astype(F32)
+        seg = jnp.broadcast_to(row, (128, 128)).T
+        start = jnp.where(
+            seg >= 3.0,
+            starts[2],
+            jnp.where(seg >= 2.0, starts[1], jnp.where(seg >= 1.0, starts[0], 0.0)),
+        )
+        pos = (iota((128, 128), 0) + base).astype(F32) - start
+        angle = pos * freq_ref[...]
+        rows = pl.ds(w * 128, 128)
+        cos_ref[rows, :] = jnp.cos(angle)
+        sin_ref[rows, :] = jnp.sin(angle) * sign
+        hit = seg == lane.astype(F32)
+        fq_ref[rows, :] = jnp.where(hit, 1.0, 0.0).astype(BF)
+        fk_ref[rows, :] = jnp.where(hit | (lane >= 4), 0.0, NEG).astype(BF)
+    gap = iota((QB, QB), 0) - iota((QB, QB), 1)
+    gap = jnp.where(flip == 1, -gap, gap)
+    bias_ref[0] = jnp.where(gap >= 0, 0.0, NEG)
+    bias_ref[1] = jnp.where(gap <= 0, 0.0, NEG)
+
+
+def qkv_rows(rb, xw, wq, aqkv, bblk, cos_ref, sin_ref, q_ref, k_ref, v_ref, low_ref):
+    rows = pl.ds(pl.multiple_of(rb * QB, QB), QB)
+    x = xw[rows, :]
+    low = nt(x, aqkv[...]).astype(BF)
+    low_ref[rows, :] = low
+    cosine = cos_ref[rows, :]
+    sine = sin_ref[rows, :]
+    for p, dest in enumerate((q_ref, k_ref, v_ref)):
+        proj = nn(x, wq[p].reshape(D, D)) + nn(low, bblk[p])
+        if p == 0:
+            value = rope(proj, cosine, sine).astype(BF) * jnp.asarray(0.125, BF)
+        elif p == 1:
+            value = rope(proj, cosine, sine).astype(BF)
+        else:
+            value = proj.astype(BF)
+        dest[rb] = value
+
+
+def attend_pair(
+    qb, pair, step, q_ref, k_ref, v_ref, fq_ref, fk_ref, bias_ref, att_ref, linv_ref, mf_ref, p_hbm, stage, sem
+):
+    k0, n, tri_first, tri_last = PLAN[qb]
+    rows = pl.ds(qb * QB, QB)
+    kblocks = pl.ds(k0, n)
+    krows = pl.ds(k0 * QB, n * QB)
+    half = iota((1, 128), 1) >= HEAD_DIM
+    lane = iota((1, 128), 1)
+    slot = lax.rem(step, 2)
+
+    def copy(s):
+        return pltpu.make_async_copy(stage.at[pl.ds(s * 4, 4)], p_hbm.at[qb, pair], sem.at[s])
+
+    @pl.when(pair >= 2)
+    def _():
+        copy(slot).wait()
+
+    lanes = pl.ds(pl.multiple_of(pair * 128, 128), 128)
+    q2 = q_ref[qb, :, lanes]
+    fq = fq_ref[rows, :]
+    keys = jnp.concatenate([k_ref[kblocks, :, lanes].reshape(n * QB, 128), fk_ref[krows, :]], axis=1)
+    v2 = v_ref[kblocks, :, lanes].reshape(n * QB, 128)
+    outs = []
+    for h in range(2):
+        mine = half if h == 1 else jnp.logical_not(half)
+        qm = jnp.where(mine, q2, jnp.zeros_like(q2))
+        s = nt(jnp.concatenate([qm, fq], axis=1), keys)
+        parts = [s[:, t * QB : (t + 1) * QB] for t in range(n)]
+        if tri_last:
+            parts[n - 1] = parts[n - 1] + bias_ref[0]
+        if tri_first:
+            parts[0] = parts[0] + bias_ref[1]
+        s = jnp.concatenate(parts, axis=1)
+        m = jnp.max(s, axis=1, keepdims=True)
+        p = jnp.exp(s - m).astype(BF)
+        for g in range((n + 2) // 3):
+            part = p[:, g * D : min(g * D + D, n * QB)]
+            stage[slot * 4 + h * 2 + g, :, 0 : part.shape[1]] = part
+        if qb >= 2:
+            low = 4 + 3 * (2 * pair + h)
+            mf_ref[rows, :] = jnp.where((lane >= low) & (lane < low + 3), -m, mf_ref[rows, :])
+        outs.append(nn(p, jnp.where(mine, v2, jnp.ones_like(v2))))
+    inv = 1.0 / pltpu.roll(jnp.where(half, outs[0], outs[1]), HEAD_DIM, 1)
+    att_ref[rows, lanes] = (jnp.where(half, outs[1], outs[0]) * inv).astype(BF)
+    linv_ref[rows, lanes] = inv
+    copy(slot).start()
+
+
+def drain_pairs(qb, p_hbm, stage, sem):
+    for s in range(2):
+        pltpu.make_async_copy(stage.at[pl.ds(s * 4, 4)], p_hbm.at[qb, 0], sem.at[s]).wait()
+
+
+def norm_stats(r):
+    centre = r - jnp.mean(r, axis=1, keepdims=True)
+    rstd = lax.rsqrt(jnp.mean(centre * centre, axis=1, keepdims=True) + EPSILON)
+    return centre * rstd, rstd
+
+
+def norm_back(grad, xhat, rstd):
+    return rstd * (
+        grad
+        - jnp.mean(grad, axis=1, keepdims=True)
+        - xhat * jnp.mean(grad * xhat, axis=1, keepdims=True)
+    )
+
+
+def out_rows(rb, xw, att_ref, wo, ao, bo, gb, aff, xhat_ref, rstd_ref, act_ref, lowo_ref, lowf_ref):
+    rows = pl.ds(pl.multiple_of(rb * QB, QB), QB)
+    att = att_ref[rows, :]
+    low = nt(att, ao[...]).astype(BF)
+    lowo_ref[rows, :] = low
+    branch = nn(att, wo[...].reshape(D, D)) + nn(low, bo[...])
+    xhat, rstd = norm_stats(xw[rows, :].astype(F32) + branch)
+    xhat_ref[rows, :] = xhat
+    rstd_ref[rows, :] = jnp.broadcast_to(rstd, (QB, 128))
+    act = (xhat * gb[0:1, :] + gb[1:2, :]).astype(BF)
+    act_ref[rows, :] = act
+    lowf_ref[rows, :] = nt(act, aff[...]).astype(BF)
+
+
+def ffn_in_tile(n, rb, size, act_ref, lowf_ref, wi, wd, bg, bu, adn, big, lowd_ref, total_ref):
+    start = pl.multiple_of(rb * size, size)
+    rows = pl.ds(start, size)
+    act = act_ref[rows, :]
+    low = lowf_ref[rows, :]
+    gate = nn(act, wi[n, 0].reshape(D, D)) + nn(low, bg[n])
+    up = nn(act, wi[n, 1].reshape(D, D)) + nn(low, bu[n])
+    inner = (gate * (1.0 / (1.0 + jnp.exp(-gate))) * up).astype(BF)
+    blocks = size // QB
+    here = n * 4 + rb * blocks
+    big[pl.ds(here, blocks)] = gate.astype(BF).reshape(blocks, QB, D)
+    big[pl.ds(here + 16, blocks)] = up.astype(BF).reshape(blocks, QB, D)
+    lowd_ref[rows, 0:16] += nt(inner, adn[n])
+    total_ref[rows, :] += nn(inner, wd[pl.ds(n * 8, 8)].reshape(D, D))
+
+
+def ffn_out_rows(
+    rb, flip, lowd_ref, bdn, xhat_ref, gb, cot, dtwo_ref, db2_ref, dlow_ref, mixed_ref, gbdn_ref
+):
+    start = pl.multiple_of(rb * QB, QB)
+    rows = pl.ds(start, QB)
+    low = lowd_ref[rows, 0:16].astype(BF)
+    total = nn(low, bdn[...]) + dtwo_ref[rows, :]
+    r = xhat_ref[rows, :] * gb[0:1, :] + gb[1:2, :] + total
+    xhat, rstd = norm_stats(r)
+    mixed_ref[pl.ds(block_at(flip, rb), QB), :] = (xhat * gb[2:3, :] + gb[3:4, :]).astype(BF)
+    dtwo = norm_back(cot[rows, :].astype(F32) * gb[2:3, :], xhat, rstd)
+    dtwo_ref[rows, :] = dtwo
+    db2 = dtwo.astype(BF)
+    db2_ref[rows, :] = db2
+    dlow_ref[rows, :] = nt(db2, bdn[...]).astype(BF)
+    gbdn_ref[...] += tn(low, db2)
+
+
+def ffn_back_tile(
+    n, start, size, db2_ref, dlow_ref, wd, wi, adn, bg, bu, big, lowf_ref, acc, dlf_ref, gadn_ref, gbf_ref
+):
+    rows = pl.ds(start, size)
+    db2 = db2_ref[rows, :]
+    dlow = dlow_ref[rows, :]
+    dinner = nt(db2, wd[pl.ds(n * 8, 8)].reshape(D, D)) + nn(dlow, adn[n])
+    blocks = size // QB
+    here = n * 4 + lax.div(start, QB)
+    gate = big[pl.ds(here, blocks)].reshape(size, D).astype(F32)
+    up = big[pl.ds(here + 16, blocks)].reshape(size, D).astype(F32)
+    sig = 1.0 / (1.0 + jnp.exp(-gate))
+    silu = gate * sig
+    inner = (silu * up).astype(BF)
+    dg = (dinner * up * (sig + silu * (1.0 - sig))).astype(BF)
+    du = (dinner * silu).astype(BF)
+    acc[...] += nt(dg, wi[n, 0].reshape(D, D)) + nt(du, wi[n, 1].reshape(D, D))
+    dlf_ref[...] += nt(dg, bg[n]) + nt(du, bu[n])
+    gadn_ref[n] += tn(dlow, inner)
+    low = lowf_ref[rows, :]
+    gbf_ref[n] += jnp.where(iota((32, 1), 0) < 16, tn(low, dg), tn(low, du))
+
+
+def hidden_back_rows(
+    rb, off, acc, dlf_ref, aff, act_ref, dtwo_ref, xhat_ref, rstd_ref, gb, bo, ao, lowo_ref, att_ref,
+    wo, linv_ref, h2, mf_ref, do_ref, hf_ref, gaff_ref, gbo_ref, gao_ref,
+):
+    start = pl.multiple_of(rb * QB, QB)
+    rows = pl.ds(start, QB)
+    local = pl.ds(pl.multiple_of(start - off, QB), QB)
+    dlf = dlf_ref[local, :].astype(BF)
+    dhid = dtwo_ref[rows, :] + acc[local, :] + nn(dlf, aff[...])
+    gaff_ref[...] += tn(dlf, act_ref[rows, :])
+    done = norm_back(dhid * gb[0:1, :], xhat_ref[rows, :], rstd_ref[rows, 0:1])
+    dtwo_ref[rows, :] = done
+    dbr = done.astype(BF)
+    dlo = nt(dbr, bo[...]).astype(BF)
+    att = att_ref[rows, :]
+    gbo_ref[...] += tn(lowo_ref[rows, :], dbr)
+    gao_ref[...] += tn(dlo, att)
+    datt = (nt(dbr, wo[...].reshape(D, D)) + nn(dlo, ao[...])).astype(BF)
+    do = (datt.astype(F32) * linv_ref[rows, :]).astype(BF)
+    do_ref[rows, :] = do
+    value = nn(do * att, h2[...]) + mf_ref[rows, :]
+    lane = iota((1, 128), 1)
+    role = jnp.where(lane < 40, lax.rem(lane + 2, 3), lax.rem(lane, 2))
+    high = value.astype(BF)
+    rest = value - high.astype(F32)
+    mid = rest.astype(BF)
+    last = (rest - mid.astype(F32)).astype(BF)
+    hf_ref[rows, :] = jnp.where(role == 0, high, jnp.where(role == 1, mid, last))
+
+
+def kf_kernel(
+    x_hbm, xh_hbm, cot_hbm, seg_ref, freq_ref, aqkv, bqkv, ao, bo, aff, bff, adn, bdn, gb,
+    wq_hbm, wo_hbm, wi_hbm, wd_hbm,
+    q_hbm, k_hbm, v_hbm, p_hbm, mixed_ref, do_ref, hf_ref, lowq_hbm, done_hbm, cos_hbm, sin_hbm, fq_hbm, fk_hbm,
+    gao_ref, gaff_ref, gadn_ref, gbo_ref, gbdn_ref, gbf_ref,
+    wq, wo, wi, wd, big, xw, att, linv, xhat, dtwo, act, db2, cos, sin, fq, fk, bias, mf,
+    lowq, lowo, lowf, dlow, acc, dlf, bblk, bg, bu, h2, wsem, xsem, osem, psem,
+):
+    flip = lax.axis_index("seq")
+    cot = db2
+    rstd = cos
+    lowd = sin
+    loads = []
+    for i in range(4):
+        loads.append(
+            pltpu.make_async_copy(
+                x_hbm.at[pl.ds(block_at(flip, i), QB)], xw.at[pl.ds(i * QB, QB)], xsem.at[i]
+            )
+        )
+        loads.append(
+            pltpu.make_async_copy(
+                cot_hbm.at[pl.ds(block_at(flip, i), QB)], cot.at[pl.ds(i * QB, QB)], xsem.at[4 + i]
+            )
+        )
+    for i in range(2):
+        at = pl.multiple_of(jnp.where(flip == 1, 1 - i, i) * QB, QB)
+        loads.append(
+            pltpu.make_async_copy(xh_hbm.at[pl.ds(at, QB)], xw.at[pl.ds(1024 + i * QB, QB)], xsem.at[8 + i])
+        )
+    weights = [
+        pltpu.make_async_copy(a, b, wsem.at[i])
+        for i, (a, b) in enumerate(((wq_hbm, wq), (wo_hbm, wo), (wi_hbm, wi), (wd_hbm, wd)))
+    ]
+    for copy in loads + weights:
+        copy.start()
+    fill_tables(flip, seg_ref, freq_ref, cos, sin, fq, fk, bias)
+    rank = iota((48, 1), 0)
+    for p in range(3):
+        keep = (rank >= 16 * p) & (rank < 16 * p + 16)
+        bblk[p] = jnp.where(keep, bqkv[...], jnp.zeros_like(bqkv[...]))
+    rank = iota((32, 1), 0)
+    for n in range(4):
+        piece = bff[:, n * D : (n + 1) * D]
+        bg[n] = jnp.where(rank < 16, piece, jnp.zeros_like(piece))
+        bu[n] = jnp.where(rank >= 16, piece, jnp.zeros_like(piece))
+    head = lax.div(iota((D, 128), 0), HEAD_DIM)
+    spot = iota((D, 128), 1)
+    h2[...] = jnp.where(lax.div(spot - 40, 2) == head, jnp.where(spot >= 40, -1.0, 0.0), 0.0).astype(BF)
+    mf[...] = jnp.zeros_like(mf)
+    dtwo[...] = jnp.zeros_like(dtwo)
+    for g in (gao_ref, gaff_ref, gadn_ref, gbo_ref, gbdn_ref, gbf_ref):
+        g[...] = jnp.zeros_like(g)
+    for copy in loads:
+        copy.wait()
+    weights[0].wait()
+    q_ref, k_ref, v_ref = (big.at[pl.ds(i * 6, 6)] for i in range(3))
+    stage = big.at[pl.ds(18, 8)]
+
+    def qkv_step(rb, _):
+        qkv_rows(rb, xw, wq, aqkv, bblk, cos, sin, q_ref, k_ref, v_ref, lowq)
+        return 0
+
+    lax.fori_loop(0, 6, qkv_step, 0)
+    saves = [
+        pltpu.make_async_copy(a, b, osem.at[i])
+        for i, (a, b) in enumerate(
+            ((q_ref, q_hbm), (k_ref, k_hbm), (v_ref, v_hbm), (lowq, lowq_hbm), (cos, cos_hbm), (sin, sin_hbm), (fq, fq_hbm), (fk, fk_hbm))
+        )
+    ]
+    for copy in saves:
+        copy.start()
+    for qb in range(4):
+
+        def pair_step(pair, _, qb=qb):
+            attend_pair(qb, pair, pair, q_ref, k_ref, v_ref, fq, fk, bias, att, linv, mf, p_hbm, stage, psem)
+            return 0
+
+        lax.fori_loop(0, 6, pair_step, 0)
+        drain_pairs(qb, p_hbm, stage, psem)
+    for copy in saves:
+        copy.wait()
+    lowd[...] = jnp.zeros_like(lowd)
+    weights[1].wait()
+
+    def out_step(rb, _):
+        out_rows(rb, xw, att, wo, ao, bo, gb, aff, xhat, rstd, act, lowo, lowf)
+        return 0
+
+    lax.fori_loop(0, 4, out_step, 0)
+    weights[2].wait()
+    weights[3].wait()
+
+    def in_step(i, _):
+        ffn_in_tile(lax.div(i, 2), lax.rem(i, 2), 512, act, lowf, wi, wd, bg, bu, adn, big, lowd, dtwo)
+        return 0
+
+    lax.fori_loop(0, 8, in_step, 0)
+
+    def down_step(rb, _):
+        ffn_out_rows(rb, flip, lowd, bdn, xhat, gb, cot, dtwo, db2, dlow, mixed_ref, gbdn_ref)
+        return 0
+
+    lax.fori_loop(0, 4, down_step, 0)
+
+    def back_step(half, _):
+        off = pl.multiple_of(half * 512, 512)
+        acc[...] = jnp.zeros_like(acc)
+        dlf[...] = jnp.zeros_like(dlf)
+
+        def tile(n, _):
+            ffn_back_tile(
+                n, off, 512, db2, dlow, wd, wi, adn, bg, bu, big, lowf, acc, dlf, gadn_ref, gbf_ref
+            )
+            return 0
+
+        lax.fori_loop(0, 4, tile, 0)
+
+        def rows(i, _):
+            hidden_back_rows(
+                half * 2 + i, off, acc, dlf, aff, act, dtwo, xhat, rstd, gb, bo, ao, lowo, att, wo, linv, h2, mf,
+                do_ref, hf_ref, gaff_ref, gbo_ref, gao_ref,
+            )
+            return 0
+
+        lax.fori_loop(0, 2, rows, 0)
+        return 0
+
+    lax.fori_loop(0, 2, back_step, 0)
+    last = pltpu.make_async_copy(dtwo, done_hbm, osem.at[8])
+    last.start()
+    last.wait()
+
+
+def k3_kernel(
+    x_hbm, q_hbm, k_hbm, v_hbm, p_hbm, do_hbm, hf_hbm, doh_hbm, hfh_hbm, lowq_hbm, done_hbm, cos_hbm, sin_hbm,
+    fq_hbm, fk_hbm, aqkv, bqkv, wq_hbm,
+    dx_ref, ga_ref, gbq_ref,
+    xw, q, k, v, do, hf, lowq, done, cos, sin, fq, fk, wq, stage, dq, dkT, dvT, bias, sem, psem,
+):
+    flip = lax.axis_index("seq")
+    table = (
+        (q_hbm, q), (k_hbm, k), (v_hbm, v), (do_hbm, do.at[pl.ds(0, 1024)]), (hf_hbm, hf.at[pl.ds(0, 1024)]),
+        (doh_hbm.at[pl.ds(256, 256)], do.at[pl.ds(1024, 256)]), (doh_hbm.at[pl.ds(0, 256)], do.at[pl.ds(1280, 256)]),
+        (hfh_hbm.at[pl.ds(256, 256)], hf.at[pl.ds(1024, 256)]), (hfh_hbm.at[pl.ds(0, 256)], hf.at[pl.ds(1280, 256)]),
+        (lowq_hbm, lowq), (done_hbm, done), (cos_hbm, cos), (sin_hbm, sin), (fq_hbm, fq), (fk_hbm, fk), (wq_hbm, wq),
+    )
+    loads = [pltpu.make_async_copy(a, b, sem.at[i]) for i, (a, b) in enumerate(table)]
+    for i in range(4):
+        loads.append(
+            pltpu.make_async_copy(
+                x_hbm.at[pl.ds(block_at(flip, i), QB)], xw.at[pl.ds(i * QB, QB)], sem.at[16 + i]
+            )
+        )
+    for copy in loads:
+        copy.start()
+    dkT[...] = jnp.zeros_like(dkT)
+    dvT[...] = jnp.zeros_like(dvT)
+    ga_ref[...] = jnp.zeros_like(ga_ref)
+    gbq_ref[...] = jnp.zeros_like(gbq_ref)
+    gap = iota((QB, QB), 0) - iota((QB, QB), 1)
+    gap = jnp.where(flip == 1, -gap, gap)
+    bias[...] = jnp.where(gap <= 0, 0.0, NEG)
+    half = iota((1, 128), 1) >= HEAD_DIM
+    for copy in loads:
+        copy.wait()
+
+    def picks(pair, first, width):
+        head = 2 * pair + lax.div(iota((128, 256), 1), 128)
+        row = iota((128, 256), 0) - first - width * head
+        return jnp.where((row >= 0) & (row < width), 1.0, 0.0).astype(BF)
+
+    for qb in range(4):
+        k0, n, _, _ = PLAN[qb]
+        own = min(4 - k0, n)
+        rows = pl.ds(qb * QB, QB)
+        krows = pl.ds(k0 * QB, n * QB)
+
+        def fetch(pair, s, qb=qb, n=n):
+            return pltpu.make_async_copy(p_hbm.at[qb, pair], stage.at[s], psem.at[s])
+
+        fetch(0, 0).start()
+
+        def pair_step(pair, _, k0=k0, n=n, own=own, rows=rows, krows=krows, fetch=fetch):
+            slot = lax.rem(pair, 2)
+            fetch(pair, slot).wait()
+
+            @pl.when(pair < 5)
+            def _():
+                fetch(pair + 1, 1 - slot).start()
+
+            lanes = pl.ds(pl.multiple_of(pair * 128, 128), 128)
+            do2 = do[rows, lanes]
+            ndl = nn(hf[rows, :], picks(pair, 40, 2))
+            k2 = k[krows, lanes]
+            v2 = v[krows, lanes]
+            qT = q[rows, lanes].T
+            doT = do2.T
+            dqs = []
+            for h in range(2):
+                mine = half if h == 1 else jnp.logical_not(half)
+                p = stage[slot, 2 * h, :, 0 : min(D, n * QB)]
+                if n > 3:
+                    p = jnp.concatenate([p, stage[slot, 2 * h + 1, :, 0 : n * QB - D]], axis=1)
+                dp = nt(jnp.where(mine, do2, jnp.zeros_like(do2)), v2)
+                d = ndl[:, h * 128 : (h + 1) * 128]
+                ds = (p.astype(F32) * (dp + jnp.concatenate([d] * (2 * n), axis=1))).astype(BF)
+                dqs.append(nn(ds, k2))
+                hr = pl.ds(pl.multiple_of(pair * 128 + h * 64, 64), 64)
+                kc = pl.ds(k0 * QB, own * QB)
+                dkT[hr, kc] += nn(qT[h * 64 : (h + 1) * 64], ds[:, 0 : own * QB])
+                dvT[hr, kc] += nn(doT[h * 64 : (h + 1) * 64], p[:, 0 : own * QB])
+            dq[rows, lanes] = jnp.where(half, dqs[1], dqs[0]) * 0.125
+            return 0
+
+        lax.fori_loop(0, 6, pair_step, 0)
+
+    for i, (k0, n) in enumerate(HALO_PLAN):
+        rows = pl.ds(1024 + i * QB, QB)
+        krows = pl.ds(k0 * QB, n * QB)
+
+        def halo_step(pair, _, k0=k0, n=n, rows=rows, krows=krows):
+            lanes = pl.ds(pl.multiple_of(pair * 128, 128), 128)
+            do2 = do[rows, lanes]
+            q2 = q[rows, lanes]
+            feats = hf[rows, :]
+            ndl = nn(feats, picks(pair, 40, 2))
+            nm = nn(feats, picks(pair, 4, 3))
+            keys = jnp.concatenate([k[krows, lanes], fk[krows, :]], axis=1)
+            v2 = v[krows, lanes]
+            qT = q2.T
+            doT = do2.T
+            for h in range(2):
+                mine = half if h == 1 else jnp.logical_not(half)
+                s = nt(jnp.concatenate([jnp.where(mine, q2, jnp.zeros_like(q2)), fq[rows, :]], axis=1), keys)
+                parts = [s[:, t * QB : (t + 1) * QB] for t in range(n)]
+                parts[0] = parts[0] + bias[...]
+                s = jnp.concatenate(parts, axis=1)
+                m = nm[:, h * 128 : (h + 1) * 128]
+                p = jnp.exp(s + jnp.concatenate([m] * (2 * n), axis=1))
+                dp = nt(jnp.where(mine, do2, jnp.zeros_like(do2)), v2)
+                d = ndl[:, h * 128 : (h + 1) * 128]
+                ds = (p * (dp + jnp.concatenate([d] * (2 * n), axis=1))).astype(BF)
+                hr = pl.ds(pl.multiple_of(pair * 128 + h * 64, 64), 64)
+                kc = pl.ds(k0 * QB, n * QB)
+                dkT[hr, kc] += nn(qT[h * 64 : (h + 1) * 64], ds)
+                dvT[hr, kc] += nn(doT[h * 64 : (h + 1) * 64], p.astype(BF))
+            return 0
+
+        lax.fori_loop(0, 6, halo_step, 0)
+
+    def row_step(rb, _):
+        start = pl.multiple_of(rb * QB, QB)
+        rows = pl.ds(start, QB)
+        cosine = cos[rows, :]
+        sine = -sin[rows, :]
+        x = xw[rows, :]
+        low = lowq[rows, :]
+        dlow = jnp.zeros((QB, 48), F32)
+        lane = lax.div(iota((1, 48), 1), 16)
+        rank = lax.div(iota((48, 1), 0), 16)
+        total = done[rows, :]
+        for p in range(3):
+            if p == 0:
+                d = rope(dq[rows, :], cosine, sine)
+            else:
+                src = (dkT, dvT)[p - 1]
+                d = jnp.concatenate(
+                    [src[pl.ds(c * 128, 128), rows].T for c in range(6)], axis=1
+                )
+                if p == 1:
+                    d = rope(d, cosine, sine)
+            d = d.astype(BF)
+            dlow += jnp.where(lane == p, nt(d, bqkv[...]), 0.0)
+            gbq_ref[...] += jnp.where(rank == p, tn(low, d), 0.0)
+            total += nt(d, wq[p].reshape(D, D))
+        dlow = dlow.astype(BF)
+        ga_ref[...] += tn(dlow, x)
+        total += nn(dlow, aqkv[...])
+        dx_ref[pl.ds(block_at(flip, rb), QB), :] = total.astype(BF)
+        return 0
+
+    lax.fori_loop(0, 4, row_step, 0)
+
+
+MESH = pl.DeviceIdType.MESH
+NCHUNK = 8
+
+
+class Gather:
+    def __init__(self, refs, sems):
+        self.wq, self.wo, self.wi, self.wd = refs
+        (self.zs, self.zr, self.xs, self.xr, self.ys, self.yr, self.ds, self.dr, self.es, self.er, self.cs, self.cr) = sems
+        b = lax.axis_index("batch")
+        self.s = lax.axis_index("seq")
+        self.core = lax.rem(b, 2)
+        self.x = lax.rem(lax.div(b, 2), 2)
+        self.z = lax.div(b, 4)
+        self.devx = (b + 2 - 4 * self.x, self.s)
+        self.devy = (b, 1 - self.s)
+        self.devc = (b + 1 - 2 * self.core, self.s)
+        self.me = self.owner(self.z, 0, 0, 0)
+
+    def owner(self, z, dx, dy, dc):
+        x = 1 - self.x if dx else self.x
+        y = 1 - self.s if dy else self.s
+        c = 1 - self.core if dc else self.core
+        return (z * 4 + x * 2 + c) * 2 + y
+
+    def devz(self, z):
+        return (z * 4 + self.x * 2 + self.core, self.s)
+
+    def zof(self, d):
+        return lax.rem(self.z + d, 4)
+
+    def view(self, c, j, half=None):
+        lanes = slice(None) if half is None else pl.ds(half * 384, 384)
+        if c == 0:
+            return self.wq.at[:, j, :, lanes]
+        if c == 1:
+            return self.wo.at[j, :, lanes]
+        if c < 6:
+            return self.wi.at[c - 2, :, j, :, lanes]
+        return self.wd.at[j, pl.ds((c - 6) * 48, 48), lanes]
+
+    def copy(self, c, j, half, dev, send, recv):
+        v = self.view(c, j, half)
+        return pltpu.make_async_remote_copy(v, v, send, recv, device_id=dev, device_id_type=MESH)
+
+    def to_z(self, c, z):
+        return self.copy(c, self.me, None, self.devz(z), self.zs.at[c, z], self.zr.at[c, self.z])
+
+    def from_z(self, c, z):
+        return self.copy(c, self.owner(z, 0, 0, 0), None, self.devz(z), self.zs.at[c, z], self.zr.at[c, z])
+
+    def on_x(self, c, z, arriving):
+        return self.copy(c, self.owner(z, arriving, 0, 0), None, self.devx, self.xs.at[c, z], self.xr.at[c, z])
+
+    def on_y(self, c, z, arriving):
+        return self.copy(c, self.owner(z, 0, arriving, 0), None, self.devy, self.ys.at[c, z], self.yr.at[c, z])
+
+    def corner_x(self, c, z, arriving):
+        return self.copy(c, self.owner(z, arriving, 1, 0), 0, self.devx, self.ds.at[c, z], self.dr.at[c, z])
+
+    def corner_y(self, c, z, arriving):
+        return self.copy(c, self.owner(z, 1, arriving, 0), 1, self.devy, self.es.at[c, z], self.er.at[c, z])
+
+    def on_core(self, c, kind, z, arriving):
+        j = self.owner(z, kind & 1, kind >> 1, arriving)
+        k = kind * 4 + z
+        return self.copy(c, j, None, self.devc, self.cs.at[c, k], self.cr.at[c, k])
+
+    def barrier(self):
+        bar = pltpu.get_barrier_semaphore()
+        for dev in (self.devx, self.devy, self.devc, self.devz(self.zof(1)), self.devz(self.zof(2)), self.devz(self.zof(3))):
+            pl.semaphore_signal(bar, inc=1, device_id=dev, device_id_type=MESH)
+        pl.semaphore_wait(bar, 6)
+
+    def stage_own(self, c):
+        self.on_x(c, self.z, 0).start()
+        self.on_y(c, self.z, 0).start()
+        for d in (1, 3, 2):
+            self.to_z(c, self.zof(d)).start()
+        self.on_core(c, 0, self.z, 0).start()
+
+    def stage_z(self, c):
+        for d in (1, 3, 2):
+            z = self.zof(d)
+            self.from_z(c, z).wait_recv()
+            self.on_x(c, z, 0).start()
+            self.on_y(c, z, 0).start()
+            self.on_core(c, 0, z, 0).start()
+
+    def stage_xy(self, c):
+        for d in range(4):
+            z = self.zof(d)
+            self.on_x(c, z, 1).wait_recv()
+            self.corner_y(c, z, 0).start()
+            self.on_core(c, 1, z, 0).start()
+            self.on_y(c, z, 1).wait_recv()
+            self.corner_x(c, z, 0).start()
+            self.on_core(c, 2, z, 0).start()
+
+    def stage_corner(self, c):
+        for d in range(4):
+            z = self.zof(d)
+            self.corner_x(c, z, 1).wait_recv()
+            self.corner_y(c, z, 1).wait_recv()
+            self.on_core(c, 3, z, 0).start()
+
+    def stage_core(self, c):
+        for kind in range(4):
+            for z in range(4):
+                self.on_core(c, kind, z, 1).wait_recv()
+
+    def finish(self, c):
+        for d in (1, 2, 3):
+            self.to_z(c, self.zof(d)).wait_send()
+        for z in range(4):
+            self.on_x(c, z, 0).wait_send()
+            self.on_y(c, z, 0).wait_send()
+            self.corner_x(c, z, 0).wait_send()
+            self.corner_y(c, z, 0).wait_send()
+            for kind in range(4):
+                self.on_core(c, kind, z, 0).wait_send()
+
+
+def gather_kernel(q, o, i, d, wq, wo, wi, wd, *rest):
+    g = Gather((wq, wo, wi, wd), rest[:12])
+    lsem = rest[12]
+    local = [
+        pltpu.make_async_copy(q, wq.at[:, g.me], lsem.at[0]),
+        pltpu.make_async_copy(o, wo.at[g.me], lsem.at[1]),
+        pltpu.make_async_copy(d, wd.at[g.me], lsem.at[2]),
+    ]
+    for n in range(4):
+        local.append(pltpu.make_async_copy(i.at[:, :, pl.ds(D * n, D)], wi.at[n, :, g.me], lsem.at[3 + n]))
+    for copy in local:
+        copy.start()
+    g.barrier()
+    for copy in local:
+        copy.wait()
+    for t in range(NCHUNK + 4):
+        for lag, stage in enumerate((g.stage_own, g.stage_z, g.stage_xy, g.stage_corner, g.stage_core)):
+            if 0 <= t - lag < NCHUNK:
+                stage(t - lag)
+    for c in range(NCHUNK):
+        g.finish(c)
+
+
+def sds(shape, dtype):
+    return jax.ShapeDtypeStruct(shape, dtype)
+
+
+ANY = functools.partial(pl.BlockSpec, memory_space=pl.ANY)
+INV = functools.partial(pl.BlockSpec, memory_space=pltpu.VMEM)
+
+
+def gather_call(q, o, i, d):
+    return pl.pallas_call(
+        gather_kernel,
+        out_shape=[sds(s, BF) for s in ((3, 32, 24, D), (32, 24, D), (4, 2, 32, 24, D), (32, 96, D))],
+        in_specs=[ANY()] * 4,
+        out_specs=[ANY()] * 4,
+        scratch_shapes=[pltpu.SemaphoreType.DMA((NCHUNK, 4))] * 10
+        + [pltpu.SemaphoreType.DMA((NCHUNK, 16))] * 2
+        + [pltpu.SemaphoreType.DMA((7,))],
+        compiler_params=pltpu.CompilerParams(collective_id=1, has_side_effects=True),
+    )(q, o, i, d)
+
+
+def kf_call(*args):
+    outs = [
+        (ANY, (6, QB, D), BF), (ANY, (6, QB, D), BF), (ANY, (6, QB, D), BF), (ANY, (4, 6, 4, QB, D), BF),
+        (INV, (1024, D), BF), (INV, (1024, D), BF), (INV, (1024, 128), BF),
+        (ANY, (1536, 48), BF), (ANY, (1024, D), F32), (ANY, (1536, 128), F32), (ANY, (1536, 128), F32),
+        (ANY, (1536, 128), BF), (ANY, (1536, 128), BF),
+        (INV, (16, D), F32), (INV, (32, D), F32), (INV, (4, 16, D), F32), (INV, (16, D), F32), (INV, (16, D), F32),
+        (INV, (4, 32, D), F32),
+    ]
+    V = pltpu.VMEM
+    scratch = [
+        V((3, 32, 24, D), BF), V((32, 24, D), BF), V((4, 2, 32, 24, D), BF), V((32, 96, D), BF),
+        V((32, QB, D), BF), V((1536, D), BF), V((1024, D), BF), V((1024, D), F32),
+        V((1024, D), F32), V((1024, D), F32), V((1024, D), BF), V((1024, D), BF),
+        V((1536, 128), F32), V((1536, 128), F32), V((1536, 128), BF), V((1536, 128), BF), V((2, QB, QB), F32),
+        V((1024, 128), F32), V((1536, 48), BF), V((1024, 16), BF), V((1024, 32), BF),
+        V((1024, 16), BF), V((512, D), F32), V((512, 32), F32), V((3, 48, D), BF),
+        V((4, 32, D), BF), V((4, 32, D), BF), V((D, 128), BF),
+        pltpu.SemaphoreType.DMA((4,)), pltpu.SemaphoreType.DMA((10,)), pltpu.SemaphoreType.DMA((9,)),
+        pltpu.SemaphoreType.DMA((2,)),
+    ]
+    return pl.pallas_call(
+        kf_kernel,
+        out_shape=[sds(s, t) for _, s, t in outs],
+        in_specs=[ANY()] * 3 + [INV()] * 11 + [ANY()] * 4,
+        out_specs=[m() for m, _, _ in outs],
+        scratch_shapes=scratch,
+        compiler_params=pltpu.CompilerParams(vmem_limit_bytes=VMEM_LIMIT),
+    )(*args)
+
+
+def k3_call(*args):
+    V = pltpu.VMEM
+    scratch = [
+        V((1024, D), BF), V((1536, D), BF), V((1536, D), BF), V((1536, D), BF), V((1536, D), BF), V((1536, 128), BF),
+        V((1536, 48), BF), V((1024, D), F32), V((1536, 128), F32), V((1536, 128), F32), V((1536, 128), BF),
+        V((1536, 128), BF), V((3, 32, 24, D), BF), V((2, 4, QB, D), BF), V((1024, D), F32), V((D, 1024), F32),
+        V((D, 1024), F32), V((QB, QB), F32), pltpu.SemaphoreType.DMA((20,)), pltpu.SemaphoreType.DMA((2,)),
+    ]
+    return pl.pallas_call(
+        k3_kernel,
+        out_shape=[sds((1024, D), BF), sds((48, D), F32), sds((48, D), F32)],
+        in_specs=[ANY()] * 15 + [INV()] * 2 + [ANY()],
+        out_specs=[INV()] * 3,
+        scratch_shapes=scratch,
+        compiler_params=pltpu.CompilerParams(vmem_limit_bytes=VMEM_LIMIT),
+    )(*args)
+
+
+def fast(
+    tokens, cotangent, segments, adapter_index, qkv_weight, out_weight, ffn_in_weight, ffn_out_weight,
+    norm_gain, norm_bias, adapt_in, adapt_down, adapt_out, adapt_ffn,
+):
+    side = lax.axis_index("seq")
+    x = tokens[0]
+    swap = [(0, 1), (1, 0)]
+    edge = lax.dynamic_slice_in_dim(x, jnp.where(side == 0, 512, 0), 512, 0)
+    halo = lax.ppermute(edge, "seq", swap)
+    e = adapter_index[0, 0]
+    pick = lambda table: lax.dynamic_index_in_dim(table[0], e, 0, False)
+    a_in = pick(adapt_in).transpose(0, 2, 1)
+    aqkv, ao, aff = a_in[0:3].reshape(48, D), a_in[3], a_in[4:6].reshape(32, D)
+    adn = pick(adapt_down).T.reshape(16, 4, D).transpose(1, 0, 2)
+    b_out = pick(adapt_out)
+    bqkv, bo, bdn = b_out[0:3].reshape(48, D), b_out[3], b_out[4]
+    bff = pick(adapt_ffn).reshape(32, FF)
+    gb = jnp.stack([norm_gain[0, 0], norm_bias[0, 0], norm_gain[0, 1], norm_bias[0, 1]])
+    freq = jnp.power(ROPE_BASE, -2.0 * jnp.arange(HEAD_DIM // 2, dtype=F32) / HEAD_DIM)
+    freq = jnp.tile(freq, 4)[None]
+    wq, wo, wi, wd = gather_call(qkv_weight[0], out_weight[0], ffn_in_weight[0], ffn_out_weight[0])
+    (
+        q, k, v, p, mixed, do, hf, lowq, done, cos, sin, fq, fk, gao, gaff, gadn, gbo, gbdn, gbf,
+    ) = kf_call(x, halo, cotangent[0], segments, freq, aqkv, bqkv, ao, bo, aff, bff, adn, bdn, gb, wq, wo, wi, wd)
+    q, k, v = (a.reshape(1536, D) for a in (q, k, v))
+    doh = lax.ppermute(do[512:], "seq", swap)
+    hfh = lax.ppermute(hf[512:], "seq", swap)
+    dx, gaq, gbq = k3_call(x, q, k, v, p, do, hf, doh, hfh, lowq, done, cos, sin, fq, fk, aqkv, bqkv, wq)
+    g_in = jnp.concatenate([gaq, gao, gaff]).reshape(6, 16, D)
+    g_dn = gadn.transpose(1, 0, 2).reshape(16, FF)
+    g_out = jnp.concatenate([gbq, gbo, gbdn]).reshape(5, 16, D)
+    g_ff = gbf.reshape(4, 2, 16, D).transpose(1, 2, 0, 3).reshape(2, 16, FF)
+    slot = (jnp.arange(ADAPTERS) == e).astype(F32)
+    spread = lambda g: slot.reshape((ADAPTERS,) + (1,) * g.ndim) * g[None]
+    g_in, g_dn, g_out, g_ff = lax.psum(tuple(spread(g) for g in (g_in, g_dn, g_out, g_ff)), ("batch", "seq"))
+    return (
+        mixed[None], dx[None], g_in.transpose(0, 1, 3, 2)[None], g_dn.transpose(0, 2, 1)[None], g_out[None], g_ff[None],
+    )
+
+
 def solution(mesh):
+    here = fast if dict(mesh.shape) == {"batch": 16, "seq": 2} else shards
     return jax.shard_map(
-        shards,
+        here,
         mesh=mesh,
         in_specs=(
             P("batch", "seq", None),

time: 1020 us -> 511 us (0.50); the launches traced: 1010 us -> 508 us
  matrix products: 482 us -> 0 us
  Pallas kernels: 0 us -> 304 us
  other arithmetic: 206 us -> 6.37 us
  waiting for transfers between devices: 225 us -> 160 us
  local copies, waits for them, and re-layouts: 66.5 us -> 18.7 us
    dot_general x57 -> x0, matrix products: 482 us -> none  [the longest x3 76.1 us: backward_group(): jnp.einsum('sqhd,skhd->shqk', query_block, key_block, preferred_element_t...]
    pallas_call x0 -> x3, Pallas kernels: none -> 304 us  [the longest x1 128 us: kf_call(): pl.pallas_call(kf_kernel, out_shape=[sds(s, t) for _, s, t in outs], in_s...]
    convert_element_type x5 -> x1, other arithmetic: 92.2 us -> 0.01 us  [fast(): slot = (jnp.arange(ADAPTERS) == e).astype(F32)]
    all_gather x4 -> x0, waiting for transfers between devices: 52 us -> none  [the longest x1 52 us: shards(): lax.all_gather(qkv_weight[layer_index], ('batch', 'seq'), axis=1, tiled=T...]
    reduce_sum x7 -> x0, other arithmetic: 48.9 us -> none  [the longest x3 46 us: forward_group(): row_total = jnp.sum(lifted, axis=-1, keepdims=True)]
    another operation x20 -> x1, other arithmetic: 28.3 us -> 0.61 us  [fast(): jnp.stack([norm_gain[0, 0], norm_bias[0, 0], norm_gain[0, 1], norm_bias[0...]
    ppermute x4 -> x3, waiting for transfers between devices: 41.5 us -> 16.7 us  [the longest x1 16.6 us: fast(): doh = lax.ppermute(do[512:], 'seq', swap)]
    broadcast_in_dim x9 -> x4, other arithmetic: 24.7 us -> 4.71 us  [the longest x1 1.36 us: fast(): g_ff[None]]
  transfers between devices with their start and end apart: 9 -> 4, of which waited for: 5 -> 2; matrix products, arithmetic and copies ran while one was open for 28% -> 3% of each run, Pallas kernels for 0% -> 22%
where the time goes in v1:
time: 511 us; the launch traced here: 508 us
  Pallas kernels  304 us (59%)
  waiting for transfers between devices  160 us (31%)
  local copies, waits for them, and re-layouts  18.7 us (4%)
  between operations  14.9 us (3%)
  other arithmetic  6.37 us (1%)
    psum x1, waiting for transfers between devices, fast(): lax.psum(tuple((spread(g) for g in (g_in, g_dn, g_out, g_ff))), ('batch',...  143 us
    pallas_call x1, Pallas kernels, kf_call(): pl.pallas_call(kf_kernel, out_shape=[sds(s, t) for _, s, t in outs], in_s...  128 us
    pallas_call x1, Pallas kernels, gather_call(): pl.pallas_call(gather_kernel, out_shape=[sds(s, BF) for s in ((3, 32, 24,...  110 us
    pallas_call x1, Pallas kernels, k3_call(): pl.pallas_call(k3_kernel, out_shape=[sds((1024, D), BF), sds((48, D), F32...  66.8 us
    ppermute x1, waiting for transfers between devices, fast(): doh = lax.ppermute(do[512:], 'seq', swap)  16.6 us
  transfers between devices with their start and end apart: 4, of which 2 were waited for; matrix products, arithmetic and copies ran while one was open for 3% of the time, Pallas kernels for 22%

profile of v1, /device:TPU:1, one launch (start us, length us, event | category | flops | bytes accessed | tf_op | source)
XLA Modules:
  0.0 508.3 jit_solution(9202247205489035879)
XLA Ops:
  7.2 1.2 dynamic-slice_bitcast_fusion
  8.4 2.1 collective-permute-start
  11.2 0.9 dynamic-slice_bitcast_fusion.1
  14.1 0.9 constant_dynamic-slice_fusion.1
  15.7 1.4 dynamic-slice_bitcast_fusion.2
  17.6 109.6 %shard_map.181 = (bf16[3,32,24,768]{3,2,1,0:T(8,128)(2,1)}, bf16[32,24,768]{2,1,0:T(8,128)(2,1)}, bf16[4,2,32,24,768]{4,3,2,1,0:T(8,128)(2,1)}, bf16[32,96,768]{2,1,0:T(8,128)(2,1)}) custom-call(bf16[3,24,768]{2,1,0:T(8,128)(2,1)} %bitcast.93, bf16[24,768]{1,0:T(8,128)(2,1)} %bitcast.94, bf16[2,24,3072]{2,1,0:T(8,128)(2,1)} %bitcast.89, bf16[96,768]{1,0:T(8,128)(2,1)} %bitcast.92), custom_call_target="tpu_custom_call" | custom-call | tf_op jit(solution)/shard_map/pallas_call | solution.py:1168
  127.3 1.5 constant_dynamic-slice_fusion
  129.4 1.6 constant_dynamic-slice_fusion.2
  131.0 128.1 %shard_map.182 = (bf16[6,256,768]{2,1,0:T(8,128)(2,1)}, bf16[6,256,768]{2,1,0:T(8,128)(2,1)}, bf16[6,256,768]{2,1,0:T(8,128)(2,1)}, bf16[4,6,4,256,768]{4,3,2,1,...) custom-call(bf16[1024,768]{1,0:T(8,128)(2,1)} %bitcast.71, ...), custom_call_target="tpu_custom_call" | custom-call | tf_op jit(solution)/shard_map/pallas_call | solution.py:1201
  259.1 1.0 slice.50
  260.1 1.3 collective-permute-start.2
  261.4 1.3 copy.27
  263.3 1.4 multiply_bitcast_fusion
  264.7 1.0 multiply_bitcast_fusion.3
  265.7 16.6 %collective-permute-done.1.doh_hbm = bf16[512,768]{1,0:T(8,128)(2,1)} collective-permute-done((bf16[512,768]{1,0:T(8,128)(2,1)S(1)}, bf16[512,768]{1,0:T(8,128)(2,1)}, u32[]{:S(2)}, u32[]{:S(2)}) %collective-permute-start.1) | collective-permute-done | bytes 786464 | tf_op jit(solution)/shard_map/ppermute | solution.py:1254
  282.3 66.8 %shard_map.183 = (bf16[1024,768]{1,0:T(8,128)(2,1)}, f32[48,768]{1,0:T(8,128)}, f32[48,768]{1,0:T(8,128)}) custom-call(bf16[1024,768]{1,0:T(8,128)(2,1)} %bitcast.72, bf16[1536,768]{1,0:T(8,128)(2,1)} %bitcast.73, bf16[1536,768]{1,0:T(8,128)(2,1)} %bitcast.74, bf16[1536,768]{1,0:T(8,128)(2,1)} %bitcast.75, ...), custom_call_target="tpu_custom_call" | custom-call | tf_op jit(solution)/shard_map/pallas_call | solution.py:1219
  349.2 1.0 pad_maximum_fusion.1
  350.2 1.1 multiply_bitcast_fusion.2
  351.3 1.2 multiply_bitcast_fusion.1
  352.6 143.4 %all-reduce.3.cloned.1.call-done = (f32[1,4,6,768,16]{3,4,2,1,0:T(8,128)}, f32[1,4,3072,16]{2,3,1,0:T(8,128)}, f32[1,4,5,16,768]{4,3,2,1,0:T(8,128)}, f32[1,4,2,16,3072]{4,3,2,1,0:T(8,128)}) async-done(((f32[1,4,6,768,16]{3,4,2,1,0:T(8,128)}, f32[1,4,3072,16]{2,3,1,0:T(8,128)}, f32[1,4,5,16,768]{4,3,2,1,0:T(8,128)}, f32[1,4,2,16,3072]{4,3,2,1,0:T(8,128)}), (f32[1,4,6,768,16]{3,4,2,1,0:T(8,128)}, ...) | async-done | bytes 4522000 | tf_op jit(solution)/shard_map/psum | solution.py:1263
  496.0 2.5 copy.34
  498.4 0.9 copy.35
  499.3 0.9 copy.36
  500.3 1.1 copy.37
  (41 shorter events, 4.5 us)
Async XLA Ops:
  7.2 8.5 %copy-start.9 = (f32[1,2,768]{2,1,0:T(2,128)S(1)}, f32[1,2,768]{2,1,0:T(2,128)}, u32[]{:S(2)}) copy-start(f32[1,2,768]{2,1,0:T(2,128)} %param.23) | copy-start | bytes 18436
  7.2 8.5 %copy-start.10 = (f32[1,2,768]{2,1,0:T(2,128)S(1)}, f32[1,2,768]{2,1,0:T(2,128)}, u32[]{:S(2)}) copy-start(f32[1,2,768]{2,1,0:T(2,128)} %param.22) | copy-start | bytes 18436
  7.2 488.8 %all-reduce.3.cloned.1.call-start = ((), (), s32[]{:S(2)}) async-start(), calls=%async_computation | async-start | bytes 9043968 | tf_op jit(solution)/shard_map/psum | solution.py:1263
  8.4 122.6 %collective-permute-start = (bf16[512,768]{1,0:T(8,128)(2,1)S(1)}, bf16[512,768]{1,0:T(8,128)(2,1)}, u32[]{:S(2)}, u32[]{:S(2)}) collective-permute-start(bf16[512,768]{1,0:T(8,128)(2,1)S(1)} %dynamic-slice_bitcast_fusion), channel_id=1, source_target_pairs={{0,1},{1,0},{2,3},{3,2},{4,5},{5,4},{6,7},{7,6},{8,9},{9,8},{10,11... | collective-permute-start | bytes 2359304 | tf_op jit(solution)/shard_map/ppermute | solution.py:1237
  259.1 3.8 copy-start
  260.1 5.6 %collective-permute-start.2 = (bf16[512,128]{1,0:T(8,128)(2,1)S(1)}, bf16[512,128]{1,0:T(8,128)(2,1)S(1)}, u32[]{:S(2)}, u32[]{:S(2)}) collective-permute-start(bf16[512,128]{1,0:T(8,128)(2,1)S(1)} %slice.50), channel_id=1, source_target_pairs={{0,1},{1,0},{2,3},{3,2},{4,5},{5,4},{6,7},{7,6},{8,9},{9,8},{10,11... | collective-permute-start | bytes 393224 | tf_op jit(solution)/shard_map/ppermute | solution.py:1255
  262.9 1.7 copy-start.4
  263.0 19.4 %collective-permute-start.1 = (bf16[512,768]{1,0:T(8,128)(2,1)S(1)}, bf16[512,768]{1,0:T(8,128)(2,1)}, u32[]{:S(2)}, u32[]{:S(2)}) collective-permute-start(bf16[512,768]{1,0:T(8,128)(2,1)S(1)} %slice.49), channel_id=1, source_target_pairs={{0,1},{1,0},{2,3},{3,2},{4,5},{5,4},{6,7},{7,6},{8,9},{9,8},{10,11... | collective-permute-start | bytes 2359304 | tf_op jit(solution)/shard_map/ppermute | solution.py:1254
  265.7 16.7 %copy-start.6 = (bf16[512,128]{1,0:T(8,128)(2,1)}, bf16[512,128]{1,0:T(8,128)(2,1)S(1)}, u32[]{:S(2)}) copy-start(bf16[512,128]{1,0:T(8,128)(2,1)S(1)} %collective-permute-done.2.hfh_hbm) | copy-start | bytes 393220
  349.1 2.2 copy-start.5
  349.2 2.2 copy-start.7
  349.2 2.2 copy-start.8
  496.0 2.5 copy-start.3
  496.0 3.4 copy-start.2
  498.4 1.8 copy-start.1
Sparse Core Ops, SparseCore 0:
  352.7 143.2 all-reduce.2
